TPU v7x, 32 devices: a whole 2x2x4 slice. The times are simulated.
32 devices in a mesh: rng: 4 (over y, x), az: 8 (over z, core).
Axes of the slice: x: 2, y: 2, z: 4, core: 2. Of those that a mesh axis runs over, the one named last changes fastest.
Arguments:
- echoes: bfloat16 [8, 2, 64, 6144], P('az', None, None, 'rng'), may hold values from -6 to 6
- owner_map: int32 [8], replicated, may hold values from 0 to 7, as said below
- band_start: int32 [24, 8, 8], P('rng', 'az'), may hold values from 0 to 1536, as said below
- interp: bfloat16 [8, 8, 3072, 256], P(None, 'az', 'rng'), may hold values from -0.375 to 0.375
- steer_phase: float32 [8, 64, 8192], P(None, None, 'az'), may hold values from -3.140625 to 3.140625
Outputs:
- focused_image: bfloat16 [3072, 2, 8192], P('rng', None, 'az')
Inputs may be any that keep to these rules, and one draw needn't show every extreme that they name: `owner_map`: the pings' slots are distinct. band_start[g, j, p] lies within 128 of (g mod 6) * 256 + 128.
All inputs are finite; a program needn't handle non-finite values.
Results may differ from a plain program's by a relative error of at most 0.01.
The roundings to bfloat16 on the way count: a program that leaves them out, or rounds other values in their place, can miss the bound.
Values may be sent and summed in bfloat16 or wider, within the bound.
A program may use at most 128 MiB of HBM per device.

v0:
```python
import jax
import jax.numpy as jnp
from jax import lax
from jax.sharding import PartitionSpec as P

GUARD = 128


def from_behind(block, axis, distance):
    devices = range(lax.axis_size(axis))
    route = [(i - distance, i) for i in devices if i - distance in devices]
    return lax.ppermute(block, axis, route)


def entering(part, axis, combine, identity):
    place = lax.axis_index(axis)
    gathered = lax.all_gather(part, axis)
    state = jnp.zeros_like(part) + jnp.asarray(identity, part.dtype)

    def one(turn, state):
        return combine(state, lax.dynamic_index_in_dim(gathered, turn, 0, False))

    return lax.fori_loop(0, place, one, state)


def padded_2(block, sides, width):
    for axis, dim in sides:
        count = lax.axis_size(axis)
        forward = [(i, i + 1) for i in range(count - 1)]
        backward = [(target, source) for source, target in forward]
        low = lax.ppermute(
            lax.slice_in_dim(block, block.shape[dim] - width, None, axis=dim), axis, forward
        )
        high = lax.ppermute(lax.slice_in_dim(block, 0, width, axis=dim), axis, backward)
        block = jnp.concatenate([low, block, high], axis=dim)
    return block


def spread(value, axis, source):
    kept = jnp.where(lax.axis_index(axis) == source, value, 0).astype(value.dtype)
    return lax.psum(kept, axis)


def apply_phase(real_part, imag_part, phase, axis_of_cells):
    cosine = jnp.cos(phase)
    sine = jnp.sin(phase)
    return jnp.stack(
        [real_part * cosine + imag_part * sine, imag_part * cosine - real_part * sine],
        axis=axis_of_cells,
    ).astype(jnp.bfloat16)


def add_terms(earlier, later):
    return earlier + later


def focus_tiles(image):
    real_part = image[:, 0].astype(jnp.float32)
    imag_part = image[:, 1].astype(jnp.float32)
    column = from_behind(image[:, :, 0], "az", -1).astype(jnp.float32)
    right_real = jnp.concatenate([real_part[:, 1:], column[:, 0:1]], axis=1)
    right_imag = jnp.concatenate([imag_part[:, 1:], column[:, 1:2]], axis=1)
    cross = jnp.sum(real_part * right_imag - imag_part * right_real, axis=0)
    power = jnp.sum(real_part * real_part + imag_part * imag_part, axis=0)
    cross, power = lax.psum((cross, power), "rng")
    slope = cross / (power + 1e-06)
    running = jnp.cumsum(slope)
    offset = entering(running[-1], "az", add_terms, jnp.float32(0.0))
    phase = offset + running - slope
    return apply_phase(real_part, imag_part, phase, 1)


def per_device(echoes, owner_map, band_start, interp, steer_phase):
    hydrophones = echoes.shape[2]
    pings = owner_map.shape[0]
    padded = padded_2(echoes, (("rng", 3),), GUARD)
    windows = jnp.stack([spread(padded[0], "az", owner_map[ping]) for ping in range(pings)])
    starts = band_start[:, 0, :]
    blocks = starts.shape[0]
    kernels = interp[:, 0]
    range_cells = kernels.shape[1]
    band = kernels.shape[2]
    kernels = kernels.reshape(pings, blocks, range_cells // blocks, band)

    def cut(window, start):
        return lax.dynamic_slice_in_dim(window, start, band, 2)

    slabs = jax.vmap(jax.vmap(cut, (None, 0)), (0, 1))(windows, starts)
    focused = jnp.einsum("pbik,pbchk->bipch", kernels, slabs, preferred_element_type=jnp.float32)
    focused = focused.astype(jnp.bfloat16).reshape(range_cells, pings * 2 * hydrophones)
    scale = 1.0 / jnp.sqrt(jnp.float32(pings * hydrophones))
    steer_re = (jnp.cos(steer_phase) * scale).astype(jnp.bfloat16)
    steer_im = (jnp.sin(steer_phase) * scale).astype(jnp.bfloat16)
    azimuth_cells = steer_phase.shape[2]
    upper = jnp.stack([steer_re, steer_im], axis=2)
    lower = jnp.stack([-steer_im, steer_re], axis=2)
    steering = jnp.stack([upper, lower], axis=1).reshape(pings * 2 * hydrophones, 2 * azimuth_cells)
    image = jnp.dot(focused, steering, preferred_element_type=jnp.float32).astype(jnp.bfloat16)
    image = image.reshape(range_cells, 2, azimuth_cells)
    return focus_tiles(focus_tiles(image))


def solution(mesh):
    in_specs = (
        P("az", None, None, "rng"),
        P(),
        P("rng", "az", None),
        P(None, "az", "rng", None),
        P(None, None, "az"),
    )
    out_specs = P("rng", None, "az")
    return jax.shard_map(
        per_device, mesh=mesh, in_specs=in_specs, out_specs=out_specs, check_vma=False
    )
```

profile of v0, /device:TPU:25, one launch (start us, length us, event | category | flops | bytes accessed | tf_op | source)
XLA Modules:
  0.0 361.2 jit_solution(2099133256523529667)
XLA Ops:
  10.6 3.1 collective-permute-start
  21.6 7.2 %broadcast_select_fusion = (bf16[1,2,64,1792]{2,1,0,3:T(2,128)(2,1)}, bf16[1,2,64,1792]{2,1,0,3:T(2,128)(2,1)S(1)}) fusion(pred[]{:T(512)S(6)} %eq.31, bf16[1,2,64,128]{2,1,0,3:T(2,128)(2,1)S(1)} %collective-permute-done.1, bf16[1,2,64,1536]{2,1,0,3:T(2,128)(2,1)} %copy.39, bf16[1,2,64,128]{2,1,0,3:T(2,128)(2,1)S(1)} %collective-permute-done), kind=kLoop, calls=%fused_computation.41 | loop fusion | flops 688128 | bytes 1376257 | tf_op jit(solution)/shard_map/jit(_where)/select_n | solution.py:40
  28.8 5.7 %broadcast_select_fusion.1 = (bf16[1,2,64,1792]{2,1,0,3:T(2,128)(2,1)}, bf16[1,2,64,1792]{2,1,0,3:T(2,128)(2,1)}, bf16[1,2,64,1792]{2,1,0,3:T(2,128)(2,1)}, bf16...) fusion(bf16[1,2,64,1792]{2,1,0,3:T(2,128)(2,1)S(1)} %get-tuple-, ...), kind=kLoop, calls=%fused_computation.42 | loop fusion | flops 1605632 | bytes 3670023 | tf_op jit(solution)/shard_map/jit(_where)/select_n | solution.py:40
  35.4 8.0 %negate_bitcast_fusion = bf16[8,64,1,1024]{3,1,0,2:T(8,128)(2,1)S(1)} fusion(f32[8,64,1024]{2,1,0:T(8,128)} %param.13), kind=kLoop, calls=%fused_computation.54 | loop fusion | flops 2621440 | bytes 3145728 | tf_op jit(solution)/shard_map/stack | solution.py:96
  43.4 7.7 %fusion.28 = (bf16[8,64,1,1024]{3,1,0,2:T(8,128)(2,1)S(1)}, bf16[8,64,1,1024]{3,1,0,2:T(8,128)(2,1)S(1)}) fusion(f32[8,64,1024]{2,1,0:T(8,128)S(1)} %copy-done.5), kind=kLoop, calls=%fused_computation.57 | loop fusion | flops 2097152 | bytes 4194304 | tf_op jit(solution)/shard_map/stack | solution.py:95
  53.8 8.5 %copy.46 = bf16[8,2,64,2,1024]{4,3,2,1,0:T(2,128)(2,1)} copy(bf16[8,2,64,2,1024]{4,2,0,3,1:T(8,128)(2,1)} %pad_maximum_fusion) | data formatting | bytes 8388608 | tf_op jit(solution)/shard_map/stack | solution.py:97
  62.4 5.7 %copy.61 = bf16[128,8,2,1024]{3,1,2,0:T(8,128)(2,1)} copy(bf16[128,8,2,1024]{3,2,1,0:T(2,128)(2,1)} %bitcast.85) | data formatting | bytes 8388608
  68.6 126.3 %all-reduce.8.cloned.1.call-done = (bf16[1,2,64,1792]{2,1,0,3:T(2,128)(2,1)}, bf16[1,2,64,1792]{2,1,0,3:T(2,128)(2,1)}, bf16[1,2,64,1792]{2,1,0,3:T(2,128)(2,1)}...) async-done(((bf16[1,2,64,1792]{2,1,0,3:T(2,128)(2,1)}, ...) | async-done | bytes 3670032 | tf_op jit(solution)/shard_map/psum | solution.py:41
  209.0 22.1 %gather_fusion = bf16[48,2,64,256]{2,1,3,0:T(2,128)(2,1)} fusion(bf16[8,2,64,1792]{2,1,0,3:T(2,128)(2,1)} %constant_dynamic-update-slice_fusion, s32[48]{0:T(128)S(1)} %reshape.128), kind=kCustom, calls=%fused_computation | custom fusion | bytes 6292224 | tf_op jit(solution)/shard_map/vmap(vmap())/gather | solution.py:86
  231.1 4.7 %fusion.22 = bf16[6,128,8,2,64]{1,4,3,2,0:T(8,128)(2,1)S(1)} fusion(bf16[8,6,128,256,1]{3,2,1,0,4:T(8,128)(2,1)S(1)} %bitcast.84, bf16[8,6,2,64,256]{3,2,4,1,0:T(2,128)(2,1)} %bitcast.88), kind=kOutput, calls=%fused_computation.52 | convolution fusion | flops 403439616 | bytes 7864320 | tf_op jit(solution)/shard_map/pbik,pbchk->bipch/dot_general | solution.py:89
  237.1 4.9 %convolution_convert_fusion = bf16[768,2048]{1,0:T(8,128)(2,1)} fusion(bf16[1024,2048]{1,0:T(8,128)(2,1)S(1)} %bitcast.86, bf16[128,8,6,128]{3,2,1,0:T(8,128)(2,1)S(1)} %bitcast.87), kind=kOutput, calls=%fused_computation.16 | convolution fusion | flops 3222798336 | bytes 8912896 | tf_op jit(solution)/shard_map/dot_general | solution.py:98
  242.0 4.8 %reshape.111 = bf16[768,2,1024]{2,1,0:T(2,128)(2,1)S(1)} reshape(bf16[768,2048]{1,0:T(8,128)(2,1)} %convolution_convert_fusion) | data formatting | bytes 6291456 | tf_op jit(solution)/shard_map/reshape | solution.py:99
  246.8 5.8 %fusion.40 = (bf16[768,1,1024]{2,1,0:T(2,128)(2,1)}, bf16[768,1,1024]{2,1,0:T(2,128)(2,1)}) fusion(bf16[768,2,1024]{2,1,0:T(2,128)(2,1)S(1)} %reshape.111), kind=kLoop, calls=%fused_computation.87 | loop fusion | bytes 6291456 | tf_op jit(solution)/shard_map/slice | solution.py:59
  252.9 5.4 %copy.59 = bf16[768,2,1]{1,0,2:T(8,128)(2,1)} copy(bf16[768,2,1]{2,1,0:T(2,128)(2,1)S(1)} %slice.134) | data formatting | bytes 6144
  261.1 4.8 %convert_bitcast_fusion.1 = (f32[768,1024]{1,0:T(8,128)S(1)}, bf16[768,1,1024]{2,0,1:T(8,128)(2,1)S(1)}, f32[768,1024]{1,0:T(8,128)S(1)}, bf16[768,1,1024]{2,0,1:T(8,128)(2,1)S(1)}) fusion(bf16[768,1,1024]{2,1,0:T(2,128)(2,1)} %get-tuple-element.99, bf16[768,1,1024]{2,1,0:T(2,128)(2,1)} %get-tuple-element.100), kind=kLoop, calls=%fused_computation.8 | loop fusion | flops 1572864 | bytes 12582912 | tf_op jit(solution)/shard_map/convert_element_type | solution.py:59
  269.6 8.0 %all-reduce.4 = (f32[1024]{0:T(1024)S(1)}, f32[1024]{0:T(1024)S(1)}) all-reduce(f32[1024]{0:T(1024)S(1)} %get-tuple-element.56, f32[1024]{0:T(1024)S(1)} %get-tuple-element.55), channel_id=1, replica_groups=mesh['rng'=4,'az'=8] {'rng'}, use_global_device_ids=true, to_apply=%region_9.10 | all-reduce | flops 2048 | bytes 16384 | tf_op jit(solution)/shard_map/psum | solution.py:65
  279.0 13.0 %all-reduce.1 = f32[8]{0:T(128)S(1)} all-reduce(f32[8]{0:T(128)S(1)} %slice_dynamic-update-slice_fusion.1), channel_id=1, replica_groups=mesh['rng'=4,'az'=8] {'az'}, use_global_device_ids=true, to_apply=%add.1 | all-reduce | flops 8 | bytes 64
  292.0 8.0 %while.20 = (s32[]{:T(128)}, f32[]{:T(128)}, s32[]{:T(128)}, f32[8]{0:T(128)S(1)}, s32[]{:T(128)}, /*index=5*/s32[]{:T(128)}, s32[]{:T(128)}) while((s32[]{:T(128)}, f32[]{:T(128)}, s32[]{:T(128)}, f32[8]{0:T(128)S(1)}, s32[]{:T(128)}, /*index=5*/s32[]{:T(128)}, s32[]{:T(128)}) %tuple.64), condition=%wide.region_15.16_spmd, body=%wide.region_14.15_spmd.sunk | while | flops 6 | bytes 135 | solution.py:23
  300.0 5.8 %convert_bitcast_fusion = (f32[768,1024]{1,0:T(8,128)}, bf16[768,1,1024]{2,0,1:T(8,128)(2,1)S(1)}, f32[768,1024]{1,0:T(8,128)}, bf16[768,1,1024]{2,0,1:T(8,128)(2,1)S(1)}) fusion(f32[1024]{0:T(1024)S(1)} %get-tuple-element.121, bf16[768,1,1024]{2,0,1:T(8,128)(2,1)} %copy-done.3, f32[1024]{0:T(1024)S(1)} %get-tuple-element.120, bf16[768,1,1024]{2,0,1:T(8,128)(2,1)} %copy-done.2), kind=kLoop, calls=%fused_computation.5 | loop fusion | flops 9437184 | bytes 12591104 | tf_op jit(solution)/shard_map/convert_element_type | solution.py:59
  305.9 5.2 %copy.55 = bf16[768,2,1]{1,0,2:T(8,128)(2,1)} copy(bf16[768,2,1]{2,0,1:T(8,128)(2,1)S(1)} %pad_maximum_fusion.3) | data formatting | bytes 6144 | tf_op jit(solution)/shard_map/squeeze | solution.py:60
  318.1 6.1 %all-reduce.3 = (f32[1024]{0:T(1024)S(1)}, f32[1024]{0:T(1024)S(1)}) all-reduce(f32[1024]{0:T(1024)S(1)} %get-tuple-element.54, f32[1024]{0:T(1024)S(1)} %get-tuple-element.53), channel_id=1, replica_groups=mesh['rng'=4,'az'=8] {'rng'}, use_global_device_ids=true, to_apply=%region_17.18 | all-reduce | flops 2048 | bytes 16384 | tf_op jit(solution)/shard_map/psum | solution.py:65
  325.7 13.0 %all-reduce.2 = f32[8]{0:T(128)S(1)} all-reduce(f32[8]{0:T(128)S(1)} %slice_dynamic-update-slice_fusion), channel_id=1, replica_groups=mesh['rng'=4,'az'=8] {'az'}, use_global_device_ids=true, to_apply=%add.2 | all-reduce | flops 8 | bytes 64
  338.7 9.1 %while.21 = (s32[]{:T(128)}, f32[]{:T(128)}, s32[]{:T(128)}, f32[8]{0:T(128)S(1)}, s32[]{:T(128)}, /*index=5*/s32[]{:T(128)}, s32[]{:T(128)}) while((s32[]{:T(128)}, f32[]{:T(128)}, s32[]{:T(128)}, f32[8]{0:T(128)S(1)}, s32[]{:T(128)}, /*index=5*/s32[]{:T(128)}, s32[]{:T(128)}) %tuple.67), condition=%wide.region_23.24_spmd, body=%wide.region_22.23_spmd.sunk | while | flops 6 | bytes 135 | solution.py:23
  349.2 4.9 %copy.51 = bf16[768,2,1024]{2,1,0:T(2,128)(2,1)} copy(bf16[768,2,1024]{2,0,1:T(8,128)(2,1)S(1)} %pad_maximum_fusion.1) | data formatting | bytes 6291456 | tf_op jit(solution)/shard_map/stack | solution.py:47
  (102 shorter events, 52.6 us)
Async XLA Ops:
  6.5 224.5 %copy-start = (bf16[8,1,768,256]{3,2,1,0:T(8,128)(2,1)S(1)}, bf16[8,1,768,256]{3,2,1,0:T(8,128)(2,1)}, u32[]{:S(2)}) copy-start(bf16[8,1,768,256]{3,2,1,0:T(8,128)(2,1)} %param.12) | copy-start | bytes 9437188
  6.5 188.3 %all-reduce.8.cloned.1.call-start = ((), (), s32[]{:S(2)}) async-start(), calls=%async_computation | async-start | bytes 14680064 | tf_op jit(solution)/shard_map/psum | solution.py:41
  10.6 11.0 %collective-permute-start = (bf16[1,2,64,128]{2,1,0,3:T(2,128)(2,1)S(1)}, bf16[1,2,64,128]{2,1,0,3:T(2,128)(2,1)S(1)}, u32[]{:S(2)}, u32[]{:S(2)}) collective-permute-start(bf16[1,2,64,128]{2,1,0,3:T(2,128)(2,1)S(1)} %get-tuple-element.112), channel_id=1, source_target_pairs={{0,8},{8,16},{16,24},{1,9},{9,17},{17,25},{2,10},{10,18},{18,26},{... | collective-permute-start | bytes 98312 | tf_op jit(solution)/shard_map/ppermute | solution.py:31
  13.7 7.9 %collective-permute-start.1 = (bf16[1,2,64,128]{2,1,0,3:T(2,128)(2,1)S(1)}, bf16[1,2,64,128]{2,1,0,3:T(2,128)(2,1)S(1)}, u32[]{:S(2)}, u32[]{:S(2)}) collective-permute-start(bf16[1,2,64,128]{2,1,0,3:T(2,128)(2,1)S(1)} %get-tuple-element.113), channel_id=1, source_target_pairs={{8,0},{16,8},{24,16},{9,1},{17,9},{25,17},{10,2},{18,10},{26,18},{... | collective-permute-start | bytes 98312 | tf_op jit(solution)/shard_map/ppermute | solution.py:34
  34.5 0.7 copy-start.13
  35.4 8.0 %copy-start.5 = (f32[8,64,1024]{2,1,0:T(8,128)S(1)}, f32[8,64,1024]{2,1,0:T(8,128)}, u32[]{:S(2)}) copy-start(f32[8,64,1024]{2,1,0:T(8,128)} %param.13) | copy-start | bytes 6291460
  62.4 5.7 %copy-start.14 = (u32[32]{0:T(128)S(1)}, u32[32]{0:T(128)}, u32[]{:S(2)}) copy-start(u32[32]{0:T(128)} %constant.72) | copy-start | bytes 388
  194.9 5.2 %copy-start.12 = (bf16[1,2,64,1792]{2,1,0,3:T(2,128)(2,1)S(1)}, bf16[1,2,64,1792]{2,1,0,3:T(2,128)(2,1)}, u32[]{:S(2)}) copy-start(bf16[1,2,64,1792]{2,1,0,3:T(2,128)(2,1)} %get-tuple-element.79) | copy-start | bytes 1376260
  194.9 6.7 %copy-start.11 = (bf16[1,2,64,1792]{2,1,0,3:T(2,128)(2,1)S(1)}, bf16[1,2,64,1792]{2,1,0,3:T(2,128)(2,1)}, u32[]{:S(2)}) copy-start(bf16[1,2,64,1792]{2,1,0,3:T(2,128)(2,1)} %get-tuple-element.80) | copy-start | bytes 1376260
  197.5 5.6 %copy-start.10 = (bf16[1,2,64,1792]{2,1,0,3:T(2,128)(2,1)S(1)}, bf16[1,2,64,1792]{2,1,0,3:T(2,128)(2,1)}, u32[]{:S(2)}) copy-start(bf16[1,2,64,1792]{2,1,0,3:T(2,128)(2,1)} %get-tuple-element.81) | copy-start | bytes 1376260
  200.1 4.4 %copy-start.9 = (bf16[1,2,64,1792]{2,1,0,3:T(2,128)(2,1)S(1)}, bf16[1,2,64,1792]{2,1,0,3:T(2,128)(2,1)}, u32[]{:S(2)}) copy-start(bf16[1,2,64,1792]{2,1,0,3:T(2,128)(2,1)} %get-tuple-element.82) | copy-start | bytes 1376260
  201.6 4.5 %copy-start.8 = (bf16[1,2,64,1792]{2,1,0,3:T(2,128)(2,1)S(1)}, bf16[1,2,64,1792]{2,1,0,3:T(2,128)(2,1)}, u32[]{:S(2)}) copy-start(bf16[1,2,64,1792]{2,1,0,3:T(2,128)(2,1)} %get-tuple-element.83) | copy-start | bytes 1376260
  203.1 4.5 %copy-start.7 = (bf16[1,2,64,1792]{2,1,0,3:T(2,128)(2,1)S(1)}, bf16[1,2,64,1792]{2,1,0,3:T(2,128)(2,1)}, u32[]{:S(2)}) copy-start(bf16[1,2,64,1792]{2,1,0,3:T(2,128)(2,1)} %get-tuple-element.84) | copy-start | bytes 1376260
  231.1 6.0 %copy-start.6 = (bf16[128,8,2,1024]{3,1,2,0:T(8,128)(2,1)S(1)}, bf16[128,8,2,1024]{3,1,2,0:T(8,128)(2,1)}, u32[]{:S(2)}) copy-start(bf16[128,8,2,1024]{3,1,2,0:T(8,128)(2,1)} %copy.61) | copy-start | bytes 12582916
  258.3 9.4 %collective-permute-start.2 = (bf16[768,2]{1,0:T(8,128)(2,1)}, bf16[768,2]{1,0:T(8,128)(2,1)S(1)}, u32[]{:S(2)}, u32[]{:S(2)}) collective-permute-start(bf16[768,2]{1,0:T(8,128)(2,1)} %bitcast.23), channel_id=1, source_target_pairs={{1,0},{2,1},{3,2},{4,3},{5,4},{6,5},{7,6},{9,8},{10,9},{11,10},{12... | collective-permute-start | bytes 9224 | tf_op jit(solution)/shard_map/ppermute | solution.py:12
  265.9 1.9 copy-start.2
  265.9 1.9 copy-start.3
  311.2 5.1 %collective-permute-start.3 = (bf16[768,2]{1,0:T(8,128)(2,1)}, bf16[768,2]{1,0:T(8,128)(2,1)S(1)}, u32[]{:S(2)}, u32[]{:S(2)}) collective-permute-start(bf16[768,2]{1,0:T(8,128)(2,1)} %bitcast.89), channel_id=1, source_target_pairs={{1,0},{2,1},{3,2},{4,3},{5,4},{6,5},{7,6},{9,8},{10,9},{11,10},{12... | collective-permute-start | bytes 9224 | tf_op jit(solution)/shard_map/ppermute | solution.py:12
  312.5 2.9 copy-start.4
  348.9 5.2 %copy-start.1 = (bf16[8,1,768,256]{3,2,1,0:T(8,128)(2,1)S(1)}, bf16[8,1,768,256]{3,2,1,0:T(8,128)(2,1)}, u32[]{:S(2)}) copy-start(bf16[8,1,768,256]{3,2,1,0:T(8,128)(2,1)} %param.12) | copy-start | bytes 9437188
Sparse Core Ops, SparseCore 0:
  34.7 160.1 all-reduce.7
where the time goes:
time: 368 us; the launch traced here: 361 us
  waiting for transfers between devices  126 us (34%)
  local copies, waits for them, and re-layouts  101 us (27%)
  other arithmetic  47.7 us (13%)
  blocking collectives  40.2 us (11%)
  between operations  18.8 us (5%)
  matrix products  9.65 us (3%)
  loops' own time  8.86 us (2%)
  starting transfers between devices  8.51 us (2%)
    psum x1, waiting for transfers between devices, spread(): return lax.psum(kept, axis)  126 us
    unnamed x45, local copies, waits for them, and re-layouts  29.6 us
    unnamed x2, blocking collectives  26.1 us
    gather x3, local copies, waits for them, and re-layouts, cut(): return lax.dynamic_slice_in_dim(window, start, band, 2)  22.3 us
    psum x2, blocking collectives, focus_tiles(): cross, power = lax.psum((cross, power), 'rng')  14.1 us
    select_n x2, other arithmetic, spread(): jnp.where(lax.axis_index(axis) == source, value, 0).astype(value.dtype)  12.9 us
    convert_element_type x2, other arithmetic, focus_tiles(): imag_part = image[:, 1].astype(jnp.float32)  10.6 us
    another operation x2, loops' own time, entering(): return lax.fori_loop(0, place, one, state)  8.86 us
  transfers between devices with their start and end apart: 5, of which 1 were waited for; matrix products, arithmetic and copies ran while one was open for 13% of the time, Pallas kernels for 0%

commit v1 on v0

v1 whole, which is shorter than its diff:
```python
import functools

import jax
import jax.numpy as jnp
from jax import lax
from jax.experimental import pallas as pl
from jax.experimental.pallas import tpu as pltpu
from jax.sharding import PartitionSpec as P

GUARD = 128
MESH = pl.DeviceIdType.MESH
RIGHT, LEFT, SIBLING, LOW, HIGH = range(5)


def sine_cosine(x):
    turns = jnp.floor(x * 0.6366197723675814 + 0.5)
    r = x - turns * 1.5703125
    r = r - turns * 4.837512969970703e-4
    r = r - turns * 7.549789948768648e-8
    quadrant = turns.astype(jnp.int32)
    r2 = r * r
    s = r + r * r2 * (-1 / 6 + r2 * (1 / 120 + r2 * (-1 / 5040 + r2 * (1 / 362880))))
    c = 1.0 + r2 * (-0.5 + r2 * (1 / 24 + r2 * (-1 / 720 + r2 * (1 / 40320))))
    odd = (quadrant & 1) == 1
    sine = jnp.where(odd, c, s)
    cosine = jnp.where(odd, s, c)
    sine = jnp.where((quadrant & 2) == 2, -sine, sine)
    cosine = jnp.where(((quadrant + 1) & 2) == 2, -cosine, cosine)
    return sine, cosine


def transposed_dot(a, b):
    return lax.dot_general(a, b, (((1,), (1,)), ((), ())), preferred_element_type=jnp.float32)


def kernel(
    n_rng, n_az, pings, blocks,
    ping_of, used, shift, echo, interp, phase,
    out_re, out_im,
    window, interp_v, phase_v, shifted, steer, focus, image, column, sums, totals,
    load_sem, send_sem, recv_sem, column_sem, sum_send, sum_recv, total_send, total_recv,
):
    rng, az = lax.axis_index("rng"), lax.axis_index("az")
    chips = n_az // 2
    chip, core = az // 2, az % 2
    width = echo.shape[1]
    rows = echo.shape[0]
    half = rows // 2
    cells = interp.shape[1]
    band = interp.shape[2]
    azimuths = phase.shape[2]
    block = cells // blocks
    step = width // blocks
    span = band + 2 * GUARD
    scale = 1.0 / (pings * half) ** 0.5

    barrier = pltpu.get_barrier_semaphore()
    for turn in range(1, n_rng):
        pl.semaphore_signal(barrier, inc=1, device_id={"rng": lax.rem(rng + turn, n_rng)}, device_id_type=MESH)
    for turn in range(1, n_az):
        pl.semaphore_signal(barrier, inc=1, device_id={"az": lax.rem(az + turn, n_az)}, device_id_type=MESH)
    pl.semaphore_wait(barrier, n_rng + n_az - 2)

    def inner(slot):
        return window.at[slot, :, pl.ds(GUARD, width)]

    def push(src, dst, sent, got, target):
        return pltpu.make_async_remote_copy(
            src_ref=src, dst_ref=dst, send_sem=sent, recv_sem=got, device_id=target, device_id_type=MESH
        )

    def along(src, slot, kind):
        target = {RIGHT: az + 2, LEFT: az - 2, SIBLING: az + 1 - 2 * core}[kind]
        return push(src, inner(slot), send_sem.at[kind, slot], recv_sem.at[0, slot], {"az": target})

    def edge_low(src, slot):
        return push(
            src.at[:, pl.ds(width - GUARD, GUARD)], window.at[slot, :, pl.ds(0, GUARD)],
            send_sem.at[LOW, slot], recv_sem.at[1, slot], {"rng": rng + 1},
        )

    def edge_high(src, slot):
        return push(
            src.at[:, pl.ds(0, GUARD)], window.at[slot, :, pl.ds(GUARD + width, GUARD)],
            send_sem.at[HIGH, slot], recv_sem.at[2, slot], {"rng": rng - 1},
        )

    def send_edges(src, slot):
        @pl.when(rng + 1 < n_rng)
        def _():
            edge_low(src, slot).start()

        @pl.when(rng > 0)
        def _():
            edge_high(src, slot).start()

    def wait_edges(slot):
        @pl.when(rng > 0)
        def _():
            edge_low(inner(slot), slot).wait_recv()

        @pl.when(rng + 1 < n_rng)
        def _():
            edge_high(inner(slot), slot).wait_recv()

    @pl.when(chip + 1 < chips)
    def _():
        along(echo, az, RIGHT).start()

    @pl.when(chip > 0)
    def _():
        along(echo, az, LEFT).start()

    along(echo, az, SIBLING).start()
    send_edges(echo, az)
    own_copy = pltpu.make_async_copy(echo, inner(az), load_sem.at[0])
    own_copy.start()
    interp_copy = pltpu.make_async_copy(interp, interp_v, load_sem.at[1])
    interp_copy.start()
    phase_copy = pltpu.make_async_copy(phase, phase_v, load_sem.at[2])
    phase_copy.start()

    @pl.when(rng == 0)
    def _():
        window[:, :, 0:GUARD] = jnp.zeros((n_az, rows, GUARD), window.dtype)

    @pl.when(rng == n_rng - 1)
    def _():
        window[:, :, GUARD + width:] = jnp.zeros((n_az, rows, GUARD), window.dtype)

    def prepare(where):
        for side in range(2):
            slot = 2 * where + side
            ping = ping_of[slot]

            def one_block(g, carry):
                part = interp_v[ping, pl.ds(g * block, block), :].astype(jnp.float32)
                if n_az != pings:
                    part = part * used[slot]
                part = jnp.concatenate([part, jnp.zeros((block, span - band), jnp.float32)], axis=1)
                part = pltpu.roll(part, shift[g, ping], 1)
                shifted[slot, pl.ds(g * block, block), :] = part.astype(jnp.bfloat16)
                return carry

            lax.fori_loop(0, blocks, one_block, 0)

            def one_rows(k, carry):
                sine, cosine = sine_cosine(phase_v[ping, pl.ds(k * 16, 16), :])
                sine, cosine = sine * scale, cosine * scale
                top = pl.ds(side * rows + k * 16, 16)
                low = pl.ds(side * rows + half + k * 16, 16)
                steer[where, top, 0:azimuths] = cosine.astype(jnp.bfloat16)
                steer[where, top, azimuths:] = sine.astype(jnp.bfloat16)
                steer[where, low, 0:azimuths] = (-sine).astype(jnp.bfloat16)
                steer[where, low, azimuths:] = cosine.astype(jnp.bfloat16)
                return carry

            lax.fori_loop(0, half // 16, one_rows, 0)

    def compute(where, first):
        for side in range(2):
            slot = 2 * where + side
            for g in range(blocks):
                got = transposed_dot(
                    shifted[slot, pl.ds(g * block, block), :], window[slot, :, pl.ds(g * step, span)]
                )
                focus[pl.ds(g * block, block), side * rows:(side + 1) * rows] = got.astype(jnp.bfloat16)

        def one_rows(k, carry):
            at = pl.ds(k * block, block)
            for part in range(2 * azimuths // 512):
                columns = pl.ds(part * 512, 512)
                got = jnp.dot(focus[at, :], steer[where, :, columns], preferred_element_type=jnp.float32)
                if first:
                    image[at, columns] = got
                else:
                    image[at, columns] = image[at, columns] + got
            return carry

        lax.fori_loop(0, blocks, one_rows, 0)

    interp_copy.wait()
    phase_copy.wait()
    prepare(chip)
    own_copy.wait()
    sibling = 2 * chip + 1 - core
    along(inner(sibling), sibling, SIBLING).wait_recv()
    send_edges(inner(sibling), sibling)
    wait_edges(az)
    wait_edges(sibling)
    compute(chip, True)

    def at_distance(distance, carry):
        sides = ((chip - distance, chip - distance >= 0, RIGHT), (chip + distance, chip + distance < chips, LEFT))
        for where, there, _ in sides:
            @pl.when(there)
            def _():
                prepare(where)

        for where, there, onward in sides:
            @pl.when(there)
            def _():
                slot = 2 * where + core
                along(inner(slot), slot, onward).wait_recv()
                more = chip + 1 < chips if onward == RIGHT else chip > 0

                @pl.when(more)
                def _():
                    along(inner(slot), slot, onward).start()

                along(inner(slot), slot, SIBLING).start()
                send_edges(inner(slot), slot)

        for where, there, _ in sides:
            @pl.when(there)
            def _():
                slot = 2 * where + 1 - core
                along(inner(slot), slot, SIBLING).wait_recv()
                send_edges(inner(slot), slot)

        for where, there, _ in sides:
            @pl.when(there)
            def _():
                wait_edges(2 * where)
                wait_edges(2 * where + 1)
                compute(where, False)

        return carry

    lax.fori_loop(1, chips, at_distance, 0)

    def one_group(k, carry):
        cross_re, cross_im, power = carry
        at = pl.ds(k * 16, 16)
        re16 = image[at, 0:azimuths].astype(jnp.bfloat16)
        im16 = image[at, azimuths:].astype(jnp.bfloat16)
        out_re[at, :] = re16
        out_im[at, :] = im16
        re, im = re16.astype(jnp.float32), im16.astype(jnp.float32)
        re_next = pltpu.roll(re, azimuths - 1, 1)
        im_next = pltpu.roll(im, azimuths - 1, 1)

        def fold(x):
            return x[0:8] + x[8:16]

        return (
            cross_re + fold(re * re_next + im * im_next),
            cross_im + fold(re * im_next - im * re_next),
            power + fold(re * re + im * im),
        )

    zero = jnp.zeros((8, azimuths), jnp.float32)
    cross_re, cross_im, power = lax.fori_loop(0, cells // 16, one_group, (zero, zero, zero))

    row16 = lax.broadcasted_iota(jnp.int32, (16, 128), 0)
    lane16 = lax.broadcasted_iota(jnp.int32, (16, 128), 1)

    def pick(row, lane):
        return jnp.where((row16 == row) & (lane16 == lane), 1.0, 0.0).astype(jnp.bfloat16)

    head = transposed_dot(pick(0, 0), out_re[:, 0:128]) + transposed_dot(pick(1, 0), out_im[:, 0:128])
    column[0] = head[0:8]
    send_column = push(
        column.at[0], column.at[1], column_sem.at[0], column_sem.at[1], {"az": lax.rem(az + n_az - 1, n_az)}
    )
    send_column.start()
    tail_re = transposed_dot(pick(0, 127), out_re[:, azimuths - 128:])
    tail_im = transposed_dot(pick(0, 127), out_im[:, azimuths - 128:])
    send_column.wait_recv()
    next_re, next_im = column[1, 0:1, :], column[1, 1:2, :]
    last_re, last_im = tail_re[0:1], tail_im[0:1]
    inside = jnp.where(az == n_az - 1, 0.0, 1.0)
    edge_re = jnp.sum(last_re * next_re + last_im * next_im, axis=1, keepdims=True) * inside
    edge_im = jnp.sum(last_re * next_im - last_im * next_re, axis=1, keepdims=True) * inside

    lane = lax.broadcasted_iota(jnp.int32, (8, azimuths), 1)
    row = lax.broadcasted_iota(jnp.int32, (8, azimuths), 0)
    at_end = lane == azimuths - 1
    cross_re = jnp.where(at_end, edge_re, jnp.sum(cross_re, axis=0, keepdims=True))
    cross_im = jnp.where(at_end, edge_im, jnp.sum(cross_im, axis=0, keepdims=True))
    power = jnp.sum(power, axis=0, keepdims=True)
    sums[rng] = jnp.where(row == 0, cross_re, jnp.where(row == 1, cross_im, power))

    def send_sums(turn):
        peer = lax.rem(rng + turn, n_rng)
        return push(sums.at[rng], sums.at[rng], sum_send.at[turn], sum_recv.at[rng], {"rng": peer})

    def take_sums(turn):
        peer = lax.rem(rng + turn, n_rng)
        return push(sums.at[peer], sums.at[peer], sum_send.at[turn], sum_recv.at[peer], {"rng": peer})

    for turn in range(1, n_rng):
        send_sums(turn).start()
    for turn in range(1, n_rng):
        take_sums(turn).wait_recv()
    total = sums[0]
    for turn in range(1, n_rng):
        total = total + sums[turn]
    cross_re, cross_im, power = total[0:1], total[1:2], total[2:3] + 1e-06
    slope = cross_im / power
    slope = slope + (cross_im * jnp.cos(slope) - cross_re * jnp.sin(slope)) / power
    slope = jnp.broadcast_to(slope, (8, azimuths))
    running = slope
    reach = 1
    while reach < azimuths:
        running = running + jnp.where(lane >= reach, pltpu.roll(running, reach, 1), 0.0)
        reach *= 2
    everything = jnp.sum(jnp.where(at_end, running, 0.0), axis=1, keepdims=True)
    totals[az] = jnp.broadcast_to(everything, (8, 128))

    def send_total(turn):
        peer = lax.rem(az + turn, n_az)
        return push(totals.at[az], totals.at[az], total_send.at[turn], total_recv.at[az], {"az": peer})

    def take_total(turn):
        peer = lax.rem(az + turn, n_az)
        return push(totals.at[peer], totals.at[peer], total_send.at[turn], total_recv.at[peer], {"az": peer})

    for turn in range(1, n_az):
        send_total(turn).start()
    for turn in range(1, n_az):
        take_total(turn).wait_recv()
    offset = jnp.zeros((8, 128), jnp.float32)
    for place in range(n_az):
        offset = offset + jnp.where(place < az, totals[place], 0.0)
    angle = offset[:, 0:1] + running - slope
    cosine, sine = jnp.cos(angle)[0:1], jnp.sin(angle)[0:1]

    def turn_rows(k, carry):
        at = pl.ds(k * 16, 16)
        re = out_re[at, :].astype(jnp.float32)
        im = out_im[at, :].astype(jnp.float32)
        out_re[at, :] = (re * cosine + im * sine).astype(jnp.bfloat16)
        out_im[at, :] = (im * cosine - re * sine).astype(jnp.bfloat16)
        return carry

    lax.fori_loop(0, cells // 16, turn_rows, 0)

    send_column.wait_send()
    for turn in range(1, n_rng):
        send_sums(turn).wait_send()
    for turn in range(1, n_az):
        send_total(turn).wait_send()

    def ended(slot, carry):
        where = slot // 2

        @pl.when(slot % 2 == core)
        def _():
            along(inner(slot), slot, SIBLING).wait_send()

            @pl.when((where <= chip) & (chip + 1 < chips))
            def _():
                along(inner(slot), slot, RIGHT).wait_send()

            @pl.when((where >= chip) & (chip > 0))
            def _():
                along(inner(slot), slot, LEFT).wait_send()

        @pl.when(rng + 1 < n_rng)
        def _():
            edge_low(inner(slot), slot).wait_send()

        @pl.when(rng > 0)
        def _():
            edge_high(inner(slot), slot).wait_send()

        return carry

    lax.fori_loop(0, n_az, ended, 0)


def per_device(echoes, owner_map, band_start, interp, steer_phase):
    n_rng, n_az = lax.axis_size("rng"), lax.axis_size("az")
    pings = owner_map.shape[0]
    blocks = band_start.shape[0]
    echo = echoes.reshape(echoes.shape[1] * echoes.shape[2], echoes.shape[3])
    interp = interp[:, 0]
    rows, width = echo.shape
    cells, band = interp.shape[1:]
    azimuths = steer_phase.shape[2]
    hits = owner_map[None, :] == jnp.arange(n_az, dtype=jnp.int32)[:, None]
    ping_of = jnp.sum(jnp.where(hits, jnp.arange(pings, dtype=jnp.int32)[None, :], 0), axis=1)
    used = jnp.any(hits, axis=1).astype(jnp.float32)
    nominal = jnp.arange(blocks, dtype=jnp.int32) * (width // blocks)
    shift = band_start[:, 0, :] - nominal[:, None]
    span = band + 2 * GUARD
    smem = pl.BlockSpec(memory_space=pltpu.SMEM)
    anywhere = pl.BlockSpec(memory_space=pl.ANY)
    vmem = pl.BlockSpec(memory_space=pltpu.VMEM)
    part = jax.ShapeDtypeStruct((cells, azimuths), jnp.bfloat16)
    dma = pltpu.SemaphoreType.DMA
    re, im = pl.pallas_call(
        functools.partial(kernel, n_rng, n_az, pings, blocks),
        out_shape=(part, part),
        in_specs=[smem, smem, smem, anywhere, anywhere, anywhere],
        out_specs=(vmem, vmem),
        scratch_shapes=[
            pltpu.VMEM((n_az, rows, width + 2 * GUARD), jnp.bfloat16),
            pltpu.VMEM(interp.shape, jnp.bfloat16),
            pltpu.VMEM(steer_phase.shape, jnp.float32),
            pltpu.VMEM((n_az, cells, span), jnp.bfloat16),
            pltpu.VMEM((n_az // 2, 2 * rows, 2 * azimuths), jnp.bfloat16),
            pltpu.VMEM((cells, 2 * rows), jnp.bfloat16),
            pltpu.VMEM((cells, 2 * azimuths), jnp.float32),
            pltpu.VMEM((2, 8, cells), jnp.float32),
            pltpu.VMEM((n_rng, 8, azimuths), jnp.float32),
            pltpu.VMEM((n_az, 8, 128), jnp.float32),
            dma((3,)), dma((5, n_az)), dma((3, n_az)), dma((2,)),
            dma((n_rng,)), dma((n_rng,)), dma((n_az,)), dma((n_az,)),
        ],
        compiler_params=pltpu.CompilerParams(
            collective_id=0, has_side_effects=True, vmem_limit_bytes=56 * 1024 * 1024
        ),
    )(ping_of, used, shift, echo, interp, steer_phase)
    return jnp.stack([re, im], axis=1)


def solution(mesh):
    in_specs = (
        P("az", None, None, "rng"),
        P(),
        P("rng", "az", None),
        P(None, "az", "rng", None),
        P(None, None, "az"),
    )
    out_specs = P("rng", None, "az")
    return jax.shard_map(
        per_device, mesh=mesh, in_specs=in_specs, out_specs=out_specs, check_vma=False
    )
```

time: 368 us -> 81.9 us (0.22)
  the two profiles are of different devices: /device:TPU:25 before, /device:TPU:0 now
where the time goes in v1:
time: 81.9 us; the launch traced here: 81.7 us
  Pallas kernels  70.7 us (86%)
  other arithmetic  6.07 us (7%)
  local copies, waits for them, and re-layouts  4.9 us (6%)
    pallas_call x1, Pallas kernels, per_device(): pl.pallas_call(functools.partial(kernel, n_rng, n_az, pings, blocks), out...  70.7 us
    another operation x1, local copies, waits for them, and re-layouts, per_device(): return jnp.stack([re, im], axis=1)  4.9 us
    another operation x1, other arithmetic, per_device(): return jnp.stack([re, im], axis=1)  2.17 us

profile of v1, /device:TPU:0, one launch (start us, length us, event | category | flops | bytes accessed | tf_op | source)
XLA Modules:
  0.0 81.7 jit_solution(15660920455082683183)
XLA Ops:
  0.0 0.8 fusion
  0.8 0.5 convert_element_type.3.used
  1.3 1.2 %select_reduce_fusion.ping_of = s32[8]{0:T(128)} fusion(s32[8]{0:T(128)} %param.6), kind=kLoop, calls=%fused_computation.2 | loop fusion | flops 184 | bytes 64 | tf_op jit(solution)/shard_map/reduce_sum | solution.py:383
  2.6 1.3 %bitcast_subtract_fusion.shift = s32[6,8]{1,0:T(8,128)} fusion(s32[6,1,8]{2,1,0:T(1,128)} %param.7, s32[6]{0:T(128)S(1)} %iota_multiply_fusion), kind=kLoop, calls=%fused_computation.1 | loop fusion | flops 48 | bytes 408 | tf_op jit(solution)/shard_map/sub | solution.py:386
  3.9 70.7 %shard_map.55 = (bf16[768,1024]{1,0:T(8,128)(2,1)}, bf16[768,1024]{1,0:T(8,128)(2,1)}) custom-call(s32[8]{0:T(128)} %select_reduce_fusion.ping_of, f32[8]{0:T(128)} %convert_element_type.3.used, s32[6,8]{1,0:T(8,128)} %bitcast_subtract_fusion.shift, bf16[128,1536]{1,0:T(8,128)(2,1)} %bitcast.9, bf16[8,768,256]{2,1,0:T(8,128)(2,1)} %bitcast.6, ...), custom_call_target="tpu_custom_call" | custom-call | tf_op jit(solution)/shard_map/pallas_call | solution.py:393
  74.6 2.2 %pad_maximum_fusion = bf16[768,2,1024]{2,0,1:T(8,128)(2,1)S(1)} fusion(bf16[768,1,1024]{2,0,1:T(8,128)(2,1)} %bitcast.8, bf16[768,1,1024]{2,0,1:T(8,128)(2,1)} %bitcast.7), kind=kLoop, calls=%fused_computation | loop fusion | flops 1572864 | bytes 6291456 | tf_op jit(solution)/shard_map/stack | solution.py:416
  76.8 4.9 %copy.7 = bf16[768,2,1024]{2,1,0:T(2,128)(2,1)} copy(bf16[768,2,1024]{2,0,1:T(8,128)(2,1)S(1)} %pad_maximum_fusion) | data formatting | bytes 6291456 | tf_op jit(solution)/shard_map/stack | solution.py:416
  (1 shorter events, 0.0 us)

commit v2 on v1

--- a/solution.py
+++ b/solution.py
@@ -35,8 +35,8 @@
 
 def kernel(
     n_rng, n_az, pings, blocks,
-    ping_of, used, shift, echo, interp, phase,
-    out_re, out_im,
+    owner, start, echo, interp, phase,
+    out_re, out_im, turn_of,
     window, interp_v, phase_v, shifted, steer, focus, image, column, sums, totals,
     load_sem, send_sem, recv_sem, column_sem, sum_send, sum_recv, total_send, total_recv,
 ):
@@ -51,7 +51,6 @@
     azimuths = phase.shape[2]
     block = cells // blocks
     step = width // blocks
-    span = band + 2 * GUARD
     scale = 1.0 / (pings * half) ** 0.5
 
     barrier = pltpu.get_barrier_semaphore()
@@ -131,18 +130,26 @@
     def prepare(where):
         for side in range(2):
             slot = 2 * where + side
-            ping = ping_of[slot]
+            ping = jnp.int32(0)
+            used = jnp.float32(0.0)
+            for p in range(pings):
+                hit = owner[p] == slot
+                ping = jnp.where(hit, p, ping)
+                used = jnp.where(hit, 1.0, used)
 
             def one_block(g, carry):
                 part = interp_v[ping, pl.ds(g * block, block), :].astype(jnp.float32)
                 if n_az != pings:
-                    part = part * used[slot]
-                part = jnp.concatenate([part, jnp.zeros((block, span - band), jnp.float32)], axis=1)
-                part = pltpu.roll(part, shift[g, ping], 1)
-                shifted[slot, pl.ds(g * block, block), :] = part.astype(jnp.bfloat16)
+                    part = part * used
+                move = start[g, 0, ping] - g * step
+                lane = lax.broadcasted_iota(jnp.int32, (block, band), 1)
+                part = pltpu.roll(part, lax.rem(move, band), 1)
+                near = lane >= move
+                shifted[slot, g, block:, :] = jnp.where(near, part, 0.0).astype(jnp.bfloat16)
+                shifted[slot, g + 1, 0:block, :] = jnp.where(near, 0.0, part).astype(jnp.bfloat16)
                 return carry
 
-            lax.fori_loop(0, blocks, one_block, 0)
+            lax.fori_loop(0, blocks, one_block, 0, unroll=2)
 
             def one_rows(k, carry):
                 sine, cosine = sine_cosine(phase_v[ping, pl.ds(k * 16, 16), :])
@@ -160,24 +167,36 @@
     def compute(where, first):
         for side in range(2):
             slot = 2 * where + side
-            for g in range(blocks):
-                got = transposed_dot(
-                    shifted[slot, pl.ds(g * block, block), :], window[slot, :, pl.ds(g * step, span)]
-                )
-                focus[pl.ds(g * block, block), side * rows:(side + 1) * rows] = got.astype(jnp.bfloat16)
-
-        def one_rows(k, carry):
-            at = pl.ds(k * block, block)
-            for part in range(2 * azimuths // 512):
-                columns = pl.ds(part * 512, 512)
-                got = jnp.dot(focus[at, :], steer[where, :, columns], preferred_element_type=jnp.float32)
-                if first:
-                    image[at, columns] = got
-                else:
-                    image[at, columns] = image[at, columns] + got
+            columns = slice(side * rows, (side + 1) * rows)
+            before = None
+            for k in range(blocks + 1):
+                low = block if k == 0 else 0
+                high = block if k == blocks else 2 * block
+                got = transposed_dot(shifted[slot, k, low:high, :], window[slot, :, k * step:(k + 1) * step])
+                if k > 0:
+                    focus[(k - 1) * block:k * block, columns] = (before + got[0:block]).astype(jnp.bfloat16)
+                before = got[block - low:]
+
+        def one_part(k, carry):
+            columns = pl.ds(k * 256, 256)
+            got = jnp.dot(focus[...], steer[where, :, columns], preferred_element_type=jnp.float32)
+            if first:
+                image[:, columns] = got
+            else:
+                image[:, columns] = image[:, columns] + got
             return carry
 
-        lax.fori_loop(0, blocks, one_rows, 0)
+        lax.fori_loop(0, 2 * azimuths // 256, one_part, 0)
+
+    def sides_at(distance):
+        left, right = chip - distance, chip + distance
+        return ((left, left >= 0, RIGHT), (right, right < chips, LEFT))
+
+    def prepare_at(distance):
+        for where, there, _ in sides_at(distance):
+            @pl.when(there)
+            def _():
+                prepare(where)
 
     interp_copy.wait()
     phase_copy.wait()
@@ -186,17 +205,10 @@
     sibling = 2 * chip + 1 - core
     along(inner(sibling), sibling, SIBLING).wait_recv()
     send_edges(inner(sibling), sibling)
-    wait_edges(az)
-    wait_edges(sibling)
-    compute(chip, True)
+    prepare_at(1)
 
     def at_distance(distance, carry):
-        sides = ((chip - distance, chip - distance >= 0, RIGHT), (chip + distance, chip + distance < chips, LEFT))
-        for where, there, _ in sides:
-            @pl.when(there)
-            def _():
-                prepare(where)
-
+        sides = sides_at(distance)
         for where, there, onward in sides:
             @pl.when(there)
             def _():
@@ -211,6 +223,12 @@
                 along(inner(slot), slot, SIBLING).start()
                 send_edges(inner(slot), slot)
 
+        @pl.when(distance == 1)
+        def _():
+            wait_edges(az)
+            wait_edges(sibling)
+            compute(chip, True)
+
         for where, there, _ in sides:
             @pl.when(there)
             def _():
@@ -225,6 +243,7 @@
                 wait_edges(2 * where + 1)
                 compute(where, False)
 
+        prepare_at(distance + 1)
         return carry
 
     lax.fori_loop(1, chips, at_distance, 0)
@@ -250,7 +269,7 @@
         )
 
     zero = jnp.zeros((8, azimuths), jnp.float32)
-    cross_re, cross_im, power = lax.fori_loop(0, cells // 16, one_group, (zero, zero, zero))
+    cross_re, cross_im, power = lax.fori_loop(0, cells // 16, one_group, (zero, zero, zero), unroll=2)
 
     row16 = lax.broadcasted_iota(jnp.int32, (16, 128), 0)
     lane16 = lax.broadcasted_iota(jnp.int32, (16, 128), 1)
@@ -324,17 +343,8 @@
     for place in range(n_az):
         offset = offset + jnp.where(place < az, totals[place], 0.0)
     angle = offset[:, 0:1] + running - slope
-    cosine, sine = jnp.cos(angle)[0:1], jnp.sin(angle)[0:1]
-
-    def turn_rows(k, carry):
-        at = pl.ds(k * 16, 16)
-        re = out_re[at, :].astype(jnp.float32)
-        im = out_im[at, :].astype(jnp.float32)
-        out_re[at, :] = (re * cosine + im * sine).astype(jnp.bfloat16)
-        out_im[at, :] = (im * cosine - re * sine).astype(jnp.bfloat16)
-        return carry
-
-    lax.fori_loop(0, cells // 16, turn_rows, 0)
+    turn_of[0] = jnp.cos(angle)
+    turn_of[1] = jnp.sin(angle)
 
     send_column.wait_send()
     for turn in range(1, n_rng):
@@ -368,6 +378,12 @@
         return carry
 
     lax.fori_loop(0, n_az, ended, 0)
+
+
+def turned(turn_of, in_re, in_im, out):
+    cosine, sine = turn_of[0, 0:1, :], turn_of[1, 0:1, :]
+    re, im = in_re[...].astype(jnp.float32), in_im[...].astype(jnp.float32)
+    out[...] = jnp.stack([re * cosine + im * sine, im * cosine - re * sine], axis=1).astype(jnp.bfloat16)
 
 
 def per_device(echoes, owner_map, band_start, interp, steer_phase):
@@ -379,27 +395,21 @@
     rows, width = echo.shape
     cells, band = interp.shape[1:]
     azimuths = steer_phase.shape[2]
-    hits = owner_map[None, :] == jnp.arange(n_az, dtype=jnp.int32)[:, None]
-    ping_of = jnp.sum(jnp.where(hits, jnp.arange(pings, dtype=jnp.int32)[None, :], 0), axis=1)
-    used = jnp.any(hits, axis=1).astype(jnp.float32)
-    nominal = jnp.arange(blocks, dtype=jnp.int32) * (width // blocks)
-    shift = band_start[:, 0, :] - nominal[:, None]
-    span = band + 2 * GUARD
     smem = pl.BlockSpec(memory_space=pltpu.SMEM)
     anywhere = pl.BlockSpec(memory_space=pl.ANY)
     vmem = pl.BlockSpec(memory_space=pltpu.VMEM)
     part = jax.ShapeDtypeStruct((cells, azimuths), jnp.bfloat16)
     dma = pltpu.SemaphoreType.DMA
-    re, im = pl.pallas_call(
+    re, im, turn_of = pl.pallas_call(
         functools.partial(kernel, n_rng, n_az, pings, blocks),
-        out_shape=(part, part),
-        in_specs=[smem, smem, smem, anywhere, anywhere, anywhere],
-        out_specs=(vmem, vmem),
+        out_shape=(part, part, jax.ShapeDtypeStruct((2, 8, azimuths), jnp.float32)),
+        in_specs=[smem, smem, anywhere, anywhere, anywhere],
+        out_specs=(vmem, vmem, vmem),
         scratch_shapes=[
             pltpu.VMEM((n_az, rows, width + 2 * GUARD), jnp.bfloat16),
             pltpu.VMEM(interp.shape, jnp.bfloat16),
             pltpu.VMEM(steer_phase.shape, jnp.float32),
-            pltpu.VMEM((n_az, cells, span), jnp.bfloat16),
+            pltpu.VMEM((n_az, blocks + 1, 2 * cells // blocks, band), jnp.bfloat16),
             pltpu.VMEM((n_az // 2, 2 * rows, 2 * azimuths), jnp.bfloat16),
             pltpu.VMEM((cells, 2 * rows), jnp.bfloat16),
             pltpu.VMEM((cells, 2 * azimuths), jnp.float32),
@@ -412,8 +422,16 @@
         compiler_params=pltpu.CompilerParams(
             collective_id=0, has_side_effects=True, vmem_limit_bytes=56 * 1024 * 1024
         ),
-    )(ping_of, used, shift, echo, interp, steer_phase)
-    return jnp.stack([re, im], axis=1)
+    )(owner_map, band_start, echo, interp, steer_phase)
+    lines = cells // 6
+    piece = pl.BlockSpec((lines, azimuths), lambda i: (i, 0))
+    return pl.pallas_call(
+        turned,
+        grid=(cells // lines,),
+        out_shape=jax.ShapeDtypeStruct((cells, 2, azimuths), jnp.bfloat16),
+        in_specs=[pl.BlockSpec((2, 8, azimuths), lambda i: (0, 0, 0)), piece, piece],
+        out_specs=pl.BlockSpec((lines, 2, azimuths), lambda i: (i, 0, 0)),
+    )(turn_of, re, im)
 
 
 def solution(mesh):

time: 81.9 us -> 71.9 us (0.88)
  other arithmetic: 6.07 us -> 0 us
  local copies, waits for them, and re-layouts: 4.9 us -> 0 us
  Pallas kernels: 70.7 us -> 71.6 us
    pallas_call x0 -> x1, Pallas kernels: none -> 8.22 us  [per_device(): pl.pallas_call(turned, grid=(cells // lines,), out_shape=jax.ShapeDtypeSt...]
    pallas_call x1, Pallas kernels: 70.7 us -> 63.4 us  [per_device(): pl.pallas_call(functools.partial(kernel, n_rng, n_az, pings, blocks), out...]
    another operation x1 -> x0, local copies, waits for them, and re-layouts: 4.9 us -> none  [per_device(): return jnp.stack([re, im], axis=1)]
    another operation x1 -> x0, other arithmetic: 2.17 us -> none  [per_device(): return jnp.stack([re, im], axis=1)]
    sub x1 -> x0, other arithmetic: 1.34 us -> none  [per_device(): shift = band_start[:, 0, :] - nominal[:, None]]
    reduce_sum x1 -> x0, other arithmetic: 1.25 us -> none  [per_device(): jnp.sum(jnp.where(hits, jnp.arange(pings, dtype=jnp.int32)[None, :], 0),...]
where the time goes in v2:
time: 71.9 us; the launch traced here: 71.7 us
  Pallas kernels  71.6 us (100%)
    pallas_call x1, Pallas kernels, per_device(): pl.pallas_call(functools.partial(kernel, n_rng, n_az, pings, blocks), out...  63.4 us
    pallas_call x1, Pallas kernels, per_device(): pl.pallas_call(turned, grid=(cells // lines,), out_shape=jax.ShapeDtypeSt...  8.22 us

profile of v2, /device:TPU:0, one launch (start us, length us, event | category | flops | bytes accessed | tf_op | source)
XLA Modules:
  0.0 71.7 jit_solution(6182738911256178032)
XLA Ops:
  0.0 63.4 %shard_map.55 = (bf16[768,1024]{1,0:T(8,128)(2,1)}, bf16[768,1024]{1,0:T(8,128)(2,1)}, f32[2,8,1024]{2,1,0:T(8,128)}) custom-call(s32[8]{0:T(128)} %owner.1, s32[6,1,8]{2,1,0:T(1,128)} %start.1, bf16[128,1536]{1,0:T(8,128)(2,1)} %bitcast.3, bf16[8,768,256]{2,1,0:T(8,128)(2,1)} %bitcast.2, f32[8,64,1024]{2,1,0:T(8,128)} %phase.1), custom_call_target="tpu_custom_call" | custom-call | tf_op jit(solution)/shard_map/pallas_call | solution.py:403
  63.4 8.2 %shard_map.56 = bf16[768,2,1024]{2,1,0:T(2,128)(2,1)} custom-call(f32[2,8,1024]{2,1,0:T(8,128)} %get-tuple-element.8.turn_of, bf16[768,1024]{1,0:T(8,128)(2,1)} %get-tuple-element.9.in_re, bf16[768,1024]{1,0:T(8,128)(2,1)} %get-tuple-element.10.in_im), custom_call_target="tpu_custom_call" | custom-call | tf_op jit(solution)/shard_map/pallas_call | solution.py:428

commit v3 on v2

--- a/solution.py
+++ b/solution.py
@@ -9,7 +9,8 @@
 
 GUARD = 128
 MESH = pl.DeviceIdType.MESH
-RIGHT, LEFT, SIBLING, LOW, HIGH = range(5)
+RIGHT, LEFT, SIBLING, LOW, HIGH = 0, 2, 4, 6, 7
+HALVES = 2
 
 
 def sine_cosine(x):
@@ -68,20 +69,24 @@
             src_ref=src, dst_ref=dst, send_sem=sent, recv_sem=got, device_id=target, device_id_type=MESH
         )
 
-    def along(src, slot, kind):
+    def along(src, slot, kind, part):
         target = {RIGHT: az + 2, LEFT: az - 2, SIBLING: az + 1 - 2 * core}[kind]
-        return push(src, inner(slot), send_sem.at[kind, slot], recv_sem.at[0, slot], {"az": target})
+        lines = pl.ds(part * half, half)
+        return push(
+            src.at[lines, :], inner(slot).at[lines, :],
+            send_sem.at[kind + part, slot], recv_sem.at[part, slot], {"az": target},
+        )
 
     def edge_low(src, slot):
         return push(
             src.at[:, pl.ds(width - GUARD, GUARD)], window.at[slot, :, pl.ds(0, GUARD)],
-            send_sem.at[LOW, slot], recv_sem.at[1, slot], {"rng": rng + 1},
+            send_sem.at[LOW, slot], recv_sem.at[HALVES, slot], {"rng": rng + 1},
         )
 
     def edge_high(src, slot):
         return push(
             src.at[:, pl.ds(0, GUARD)], window.at[slot, :, pl.ds(GUARD + width, GUARD)],
-            send_sem.at[HIGH, slot], recv_sem.at[2, slot], {"rng": rng - 1},
+            send_sem.at[HIGH, slot], recv_sem.at[HALVES + 1, slot], {"rng": rng - 1},
         )
 
     def send_edges(src, slot):
@@ -102,15 +107,17 @@
         def _():
             edge_high(inner(slot), slot).wait_recv()
 
-    @pl.when(chip + 1 < chips)
-    def _():
-        along(echo, az, RIGHT).start()
-
-    @pl.when(chip > 0)
-    def _():
-        along(echo, az, LEFT).start()
-
-    along(echo, az, SIBLING).start()
+    for part in range(HALVES):
+        @pl.when(chip + 1 < chips)
+        def _():
+            along(echo, az, RIGHT, part).start()
+
+        @pl.when(chip > 0)
+        def _():
+            along(echo, az, LEFT, part).start()
+
+        along(echo, az, SIBLING, part).start()
+
     send_edges(echo, az)
     own_copy = pltpu.make_async_copy(echo, inner(az), load_sem.at[0])
     own_copy.start()
@@ -198,52 +205,70 @@
             def _():
                 prepare(where)
 
+    def sides_at(distance):
+        left, right = chip - distance, chip + distance
+        return ((left, left >= 0, RIGHT), (right, right < chips, LEFT))
+
+    def forward(distance, part):
+        for where, there, onward in sides_at(distance):
+            @pl.when(there)
+            def _():
+                slot = 2 * where + core
+                along(inner(slot), slot, onward, part).wait_recv()
+                more = chip + 1 < chips if onward == RIGHT else chip > 0
+
+                @pl.when(more)
+                def _():
+                    along(inner(slot), slot, onward, part).start()
+
+                along(inner(slot), slot, SIBLING, part).start()
+                if part == HALVES - 1:
+                    send_edges(inner(slot), slot)
+
+    def from_sibling(where):
+        slot = 2 * where + 1 - core
+        for part in range(HALVES):
+            along(inner(slot), slot, SIBLING, part).wait_recv()
+        send_edges(inner(slot), slot)
+
+    def finish(where, first):
+        wait_edges(2 * where)
+        wait_edges(2 * where + 1)
+        compute(where, first)
+
     interp_copy.wait()
     phase_copy.wait()
     prepare(chip)
     own_copy.wait()
-    sibling = 2 * chip + 1 - core
-    along(inner(sibling), sibling, SIBLING).wait_recv()
-    send_edges(inner(sibling), sibling)
-    prepare_at(1)
+    from_sibling(chip)
+    finish(chip, True)
+    between = (chip > 0) & (chip + 1 < chips)
 
     def at_distance(distance, carry):
+        forward(distance, 0)
+        early = (distance == 1) | jnp.logical_not(between)
         sides = sides_at(distance)
-        for where, there, onward in sides:
-            @pl.when(there)
-            def _():
-                slot = 2 * where + core
-                along(inner(slot), slot, onward).wait_recv()
-                more = chip + 1 < chips if onward == RIGHT else chip > 0
-
-                @pl.when(more)
-                def _():
-                    along(inner(slot), slot, onward).start()
-
-                along(inner(slot), slot, SIBLING).start()
-                send_edges(inner(slot), slot)
-
-        @pl.when(distance == 1)
-        def _():
-            wait_edges(az)
-            wait_edges(sibling)
-            compute(chip, True)
+        for where, there, _ in sides:
+            @pl.when(there & early)
+            def _():
+                prepare(where)
+
+        forward(distance, 1)
+        for where, there, _ in sides:
+            @pl.when(there & jnp.logical_not(early))
+            def _():
+                prepare(where)
 
         for where, there, _ in sides:
             @pl.when(there)
             def _():
-                slot = 2 * where + 1 - core
-                along(inner(slot), slot, SIBLING).wait_recv()
-                send_edges(inner(slot), slot)
+                from_sibling(where)
 
         for where, there, _ in sides:
             @pl.when(there)
             def _():
-                wait_edges(2 * where)
-                wait_edges(2 * where + 1)
-                compute(where, False)
-
-        prepare_at(distance + 1)
+                finish(where, False)
+
         return carry
 
     lax.fori_loop(1, chips, at_distance, 0)
@@ -354,18 +379,18 @@
 
     def ended(slot, carry):
         where = slot // 2
-
-        @pl.when(slot % 2 == core)
-        def _():
-            along(inner(slot), slot, SIBLING).wait_send()
-
-            @pl.when((where <= chip) & (chip + 1 < chips))
-            def _():
-                along(inner(slot), slot, RIGHT).wait_send()
-
-            @pl.when((where >= chip) & (chip > 0))
-            def _():
-                along(inner(slot), slot, LEFT).wait_send()
+        for part in range(HALVES):
+            @pl.when(slot % 2 == core)
+            def _():
+                along(inner(slot), slot, SIBLING, part).wait_send()
+
+                @pl.when((where <= chip) & (chip + 1 < chips))
+                def _():
+                    along(inner(slot), slot, RIGHT, part).wait_send()
+
+                @pl.when((where >= chip) & (chip > 0))
+                def _():
+                    along(inner(slot), slot, LEFT, part).wait_send()
 
         @pl.when(rng + 1 < n_rng)
         def _():
@@ -380,10 +405,26 @@
     lax.fori_loop(0, n_az, ended, 0)
 
 
-def turned(turn_of, in_re, in_im, out):
+def turned(turn_of, in_re, in_im, out, new_re, new_im):
+    lines, azimuths = in_re.shape
     cosine, sine = turn_of[0, 0:1, :], turn_of[1, 0:1, :]
-    re, im = in_re[...].astype(jnp.float32), in_im[...].astype(jnp.float32)
-    out[...] = jnp.stack([re * cosine + im * sine, im * cosine - re * sine], axis=1).astype(jnp.bfloat16)
+
+    def rotate(k, carry):
+        at = pl.ds(k * 16, 16)
+        re, im = in_re[at, :].astype(jnp.float32), in_im[at, :].astype(jnp.float32)
+        new_re[at, :] = re * cosine + im * sine
+        new_im[at, :] = im * cosine - re * sine
+        return carry
+
+    lax.fori_loop(0, lines // 16, rotate, 0, unroll=2)
+    real = lax.broadcasted_iota(jnp.int32, (2, azimuths), 0) == 0
+
+    def place(k, carry):
+        pair = jnp.where(real, new_re[pl.ds(k, 1), :], new_im[pl.ds(k, 1), :])
+        out[k] = pair.astype(jnp.bfloat16)
+        return carry
+
+    lax.fori_loop(0, lines, place, 0, unroll=16)
 
 
 def per_device(echoes, owner_map, band_start, interp, steer_phase):
@@ -416,7 +457,7 @@
             pltpu.VMEM((2, 8, cells), jnp.float32),
             pltpu.VMEM((n_rng, 8, azimuths), jnp.float32),
             pltpu.VMEM((n_az, 8, 128), jnp.float32),
-            dma((3,)), dma((5, n_az)), dma((3, n_az)), dma((2,)),
+            dma((3,)), dma((3 * HALVES + 2, n_az)), dma((HALVES + 2, n_az)), dma((2,)),
             dma((n_rng,)), dma((n_rng,)), dma((n_az,)), dma((n_az,)),
         ],
         compiler_params=pltpu.CompilerParams(
@@ -431,6 +472,7 @@
         out_shape=jax.ShapeDtypeStruct((cells, 2, azimuths), jnp.bfloat16),
         in_specs=[pl.BlockSpec((2, 8, azimuths), lambda i: (0, 0, 0)), piece, piece],
         out_specs=pl.BlockSpec((lines, 2, azimuths), lambda i: (i, 0, 0)),
+        scratch_shapes=[pltpu.VMEM((lines, azimuths), jnp.float32)] * 2,
     )(turn_of, re, im)
 
 

time: 71.9 us -> 73.5 us (1.022)
  Pallas kernels: 71.6 us -> 73.3 us
    pallas_call x1, Pallas kernels: 63.4 us -> 65 us  [per_device(): pl.pallas_call(functools.partial(kernel, n_rng, n_az, pings, blocks), out...]
where the time goes in v3:
time: 73.5 us; the launch traced here: 73.3 us
  Pallas kernels  73.3 us (100%)
    pallas_call x1, Pallas kernels, per_device(): pl.pallas_call(functools.partial(kernel, n_rng, n_az, pings, blocks), out...  65 us
    pallas_call x1, Pallas kernels, per_device(): pl.pallas_call(turned, grid=(cells // lines,), out_shape=jax.ShapeDtypeSt...  8.25 us

profile of v3, /device:TPU:0, one launch (start us, length us, event | category | flops | bytes accessed | tf_op | source)
XLA Modules:
  0.0 73.3 jit_solution(10371801104830668920)
XLA Ops:
  0.0 65.0 %shard_map.55 = (bf16[768,1024]{1,0:T(8,128)(2,1)}, bf16[768,1024]{1,0:T(8,128)(2,1)}, f32[2,8,1024]{2,1,0:T(8,128)}) custom-call(s32[8]{0:T(128)} %owner.1, s32[6,1,8]{2,1,0:T(1,128)} %start.1, bf16[128,1536]{1,0:T(8,128)(2,1)} %bitcast.3, bf16[8,768,256]{2,1,0:T(8,128)(2,1)} %bitcast.2, f32[8,64,1024]{2,1,0:T(8,128)} %phase.1), custom_call_target="tpu_custom_call" | custom-call | tf_op jit(solution)/shard_map/pallas_call | solution.py:444
  65.0 8.3 %shard_map.56 = bf16[768,2,1024]{2,1,0:T(2,128)(2,1)} custom-call(f32[2,8,1024]{2,1,0:T(8,128)} %get-tuple-element.8.turn_of, bf16[768,1024]{1,0:T(8,128)(2,1)} %get-tuple-element.9.in_re, bf16[768,1024]{1,0:T(8,128)(2,1)} %get-tuple-element.10.in_im), custom_call_target="tpu_custom_call" | custom-call | tf_op jit(solution)/shard_map/pallas_call | solution.py:469

commit v4 on v3

--- a/solution.py
+++ b/solution.py
@@ -54,6 +54,13 @@
     step = width // blocks
     scale = 1.0 / (pings * half) ** 0.5
 
+    own_copy = pltpu.make_async_copy(echo, window.at[az, :, pl.ds(GUARD, width)], load_sem.at[0])
+    own_copy.start()
+    interp_copy = pltpu.make_async_copy(interp, interp_v, load_sem.at[1])
+    interp_copy.start()
+    phase_copy = pltpu.make_async_copy(phase, phase_v, load_sem.at[2])
+    phase_copy.start()
+
     barrier = pltpu.get_barrier_semaphore()
     for turn in range(1, n_rng):
         pl.semaphore_signal(barrier, inc=1, device_id={"rng": lax.rem(rng + turn, n_rng)}, device_id_type=MESH)
@@ -70,7 +77,7 @@
         )
 
     def along(src, slot, kind, part):
-        target = {RIGHT: az + 2, LEFT: az - 2, SIBLING: az + 1 - 2 * core}[kind]
+        target = az + 1 - 2 * core if kind is SIBLING else az + 2 - 2 * kind
         lines = pl.ds(part * half, half)
         return push(
             src.at[lines, :], inner(slot).at[lines, :],
@@ -107,24 +114,23 @@
         def _():
             edge_high(inner(slot), slot).wait_recv()
 
+    def directions():
+        for turn in range(2):
+            sign = 1 - 2 * ((core + turn) % 2)
+            onward = chip + sign
+            yield sign, 1 - sign, (onward >= 0) & (onward < chips)
+
+    def send_own(part):
+        for _, kind, more in directions():
+            @pl.when(more)
+            def _():
+                along(echo, az, kind, part).start()
+
+    send_own(0)
     for part in range(HALVES):
-        @pl.when(chip + 1 < chips)
-        def _():
-            along(echo, az, RIGHT, part).start()
-
-        @pl.when(chip > 0)
-        def _():
-            along(echo, az, LEFT, part).start()
-
         along(echo, az, SIBLING, part).start()
-
     send_edges(echo, az)
-    own_copy = pltpu.make_async_copy(echo, inner(az), load_sem.at[0])
-    own_copy.start()
-    interp_copy = pltpu.make_async_copy(interp, interp_v, load_sem.at[1])
-    interp_copy.start()
-    phase_copy = pltpu.make_async_copy(phase, phase_v, load_sem.at[2])
-    phase_copy.start()
+    send_own(1)
 
     @pl.when(rng == 0)
     def _():
@@ -196,30 +202,20 @@
         lax.fori_loop(0, 2 * azimuths // 256, one_part, 0)
 
     def sides_at(distance):
-        left, right = chip - distance, chip + distance
-        return ((left, left >= 0, RIGHT), (right, right < chips, LEFT))
-
-    def prepare_at(distance):
-        for where, there, _ in sides_at(distance):
+        for sign, kind, more in directions():
+            where = chip - sign * distance
+            yield where, (where >= 0) & (where < chips), kind, more
+
+    def forward(distance, part):
+        for where, there, kind, more in sides_at(distance):
             @pl.when(there)
             def _():
-                prepare(where)
-
-    def sides_at(distance):
-        left, right = chip - distance, chip + distance
-        return ((left, left >= 0, RIGHT), (right, right < chips, LEFT))
-
-    def forward(distance, part):
-        for where, there, onward in sides_at(distance):
-            @pl.when(there)
-            def _():
                 slot = 2 * where + core
-                along(inner(slot), slot, onward, part).wait_recv()
-                more = chip + 1 < chips if onward == RIGHT else chip > 0
+                along(inner(slot), slot, kind, part).wait_recv()
 
                 @pl.when(more)
                 def _():
-                    along(inner(slot), slot, onward, part).start()
+                    along(inner(slot), slot, kind, part).start()
 
                 along(inner(slot), slot, SIBLING, part).start()
                 if part == HALVES - 1:
@@ -247,24 +243,24 @@
     def at_distance(distance, carry):
         forward(distance, 0)
         early = (distance == 1) | jnp.logical_not(between)
-        sides = sides_at(distance)
-        for where, there, _ in sides:
+        sides = [(where, there) for where, there, _, _ in sides_at(distance)]
+        for where, there in sides:
             @pl.when(there & early)
             def _():
                 prepare(where)
 
         forward(distance, 1)
-        for where, there, _ in sides:
+        for where, there in sides:
             @pl.when(there & jnp.logical_not(early))
             def _():
                 prepare(where)
 
-        for where, there, _ in sides:
+        for where, there in sides:
             @pl.when(there)
             def _():
                 from_sibling(where)
 
-        for where, there, _ in sides:
+        for where, there in sides:
             @pl.when(there)
             def _():
                 finish(where, False)
@@ -405,26 +401,16 @@
     lax.fori_loop(0, n_az, ended, 0)
 
 
-def turned(turn_of, in_re, in_im, out, new_re, new_im):
+def turned(turn_of, in_re, in_im, out, mixed):
     lines, azimuths = in_re.shape
-    cosine, sine = turn_of[0, 0:1, :], turn_of[1, 0:1, :]
-
-    def rotate(k, carry):
-        at = pl.ds(k * 16, 16)
-        re, im = in_re[at, :].astype(jnp.float32), in_im[at, :].astype(jnp.float32)
-        new_re[at, :] = re * cosine + im * sine
-        new_im[at, :] = im * cosine - re * sine
-        return carry
-
-    lax.fori_loop(0, lines // 16, rotate, 0, unroll=2)
-    real = lax.broadcasted_iota(jnp.int32, (2, azimuths), 0) == 0
-
-    def place(k, carry):
-        pair = jnp.where(real, new_re[pl.ds(k, 1), :], new_im[pl.ds(k, 1), :])
-        out[k] = pair.astype(jnp.bfloat16)
-        return carry
-
-    lax.fori_loop(0, lines, place, 0, unroll=16)
+    tiles = azimuths // 128
+    for t in range(tiles):
+        lanes = slice(t * 128, (t + 1) * 128)
+        cosine, sine = turn_of[0, 0:1, lanes], turn_of[1, 0:1, lanes]
+        re, im = in_re[:, lanes].astype(jnp.float32), in_im[:, lanes].astype(jnp.float32)
+        mixed[pl.ds(2 * t, lines, stride=2 * tiles), :] = re * cosine + im * sine
+        mixed[pl.ds(2 * t + 1, lines, stride=2 * tiles), :] = im * cosine - re * sine
+    out[...] = mixed[...].astype(jnp.bfloat16)
 
 
 def per_device(echoes, owner_map, band_start, interp, steer_phase):
@@ -465,15 +451,18 @@
         ),
     )(owner_map, band_start, echo, interp, steer_phase)
     lines = cells // 6
+    tiles = azimuths // 128
     piece = pl.BlockSpec((lines, azimuths), lambda i: (i, 0))
-    return pl.pallas_call(
+    mixed = pl.pallas_call(
         turned,
         grid=(cells // lines,),
-        out_shape=jax.ShapeDtypeStruct((cells, 2, azimuths), jnp.bfloat16),
+        out_shape=jax.ShapeDtypeStruct((cells * 2 * tiles, 128), jnp.bfloat16),
         in_specs=[pl.BlockSpec((2, 8, azimuths), lambda i: (0, 0, 0)), piece, piece],
-        out_specs=pl.BlockSpec((lines, 2, azimuths), lambda i: (i, 0, 0)),
-        scratch_shapes=[pltpu.VMEM((lines, azimuths), jnp.float32)] * 2,
+        out_specs=pl.BlockSpec((lines * 2 * tiles, 128), lambda i: (i, 0)),
+        scratch_shapes=[pltpu.VMEM((lines * 2 * tiles, 128), jnp.float32)],
     )(turn_of, re, im)
+    mixed = mixed.reshape(cells, tiles, 2, 128)
+    return jnp.transpose(mixed, (0, 2, 1, 3)).reshape(cells, 2, azimuths)
 
 
 def solution(mesh):

time: 73.5 us -> 69.9 us (0.951)
  Pallas kernels: 73.3 us -> 69.6 us
    pallas_call x1, Pallas kernels: 65 us -> 62.5 us  [per_device(): pl.pallas_call(functools.partial(kernel, n_rng, n_az, pings, blocks), out...]
    pallas_call x1, Pallas kernels: 8.25 us -> 7.11 us  [per_device(): pl.pallas_call(turned, grid=(cells // lines,), out_shape=jax.ShapeDtypeSt...]
where the time goes in v4:
time: 69.9 us; the launch traced here: 69.6 us
  Pallas kernels  69.6 us (100%)
    pallas_call x1, Pallas kernels, per_device(): pl.pallas_call(functools.partial(kernel, n_rng, n_az, pings, blocks), out...  62.5 us
    pallas_call x1, Pallas kernels, per_device(): pl.pallas_call(turned, grid=(cells // lines,), out_shape=jax.ShapeDtypeSt...  7.11 us

profile of v4, /device:TPU:0, one launch (start us, length us, event | category | flops | bytes accessed | tf_op | source)
XLA Modules:
  0.0 69.6 jit_solution(502788809882368848)
XLA Ops:
  0.0 62.5 %shard_map.55 = (bf16[768,1024]{1,0:T(8,128)(2,1)}, bf16[768,1024]{1,0:T(8,128)(2,1)}, f32[2,8,1024]{2,1,0:T(8,128)}) custom-call(s32[8]{0:T(128)} %owner.1, s32[6,1,8]{2,1,0:T(1,128)} %start.1, bf16[128,1536]{1,0:T(8,128)(2,1)} %bitcast.8, bf16[8,768,256]{2,1,0:T(8,128)(2,1)} %bitcast.7, f32[8,64,1024]{2,1,0:T(8,128)} %phase.1), custom_call_target="tpu_custom_call" | custom-call | tf_op jit(solution)/shard_map/pallas_call | solution.py:430
  62.5 7.1 %shard_map.56 = bf16[12288,128]{1,0:T(8,128)(2,1)} custom-call(f32[2,8,1024]{2,1,0:T(8,128)} %get-tuple-element.8.turn_of, bf16[768,1024]{1,0:T(8,128)(2,1)} %get-tuple-element.9.in_re, bf16[768,1024]{1,0:T(8,128)(2,1)} %get-tuple-element.10.in_im), custom_call_target="tpu_custom_call" | custom-call | tf_op jit(solution)/shard_map/pallas_call | solution.py:456

commit v5 on v4

--- a/solution.py
+++ b/solution.py
@@ -37,7 +37,8 @@
 def kernel(
     n_rng, n_az, pings, blocks,
     owner, start, echo, interp, phase,
-    out_re, out_im, turn_of,
+    given_re, given_im, turn_of,
+    out_re, out_im,
     window, interp_v, phase_v, shifted, steer, focus, image, column, sums, totals,
     load_sem, send_sem, recv_sem, column_sem, sum_send, sum_recv, total_send, total_recv,
 ):
@@ -241,7 +242,6 @@
     between = (chip > 0) & (chip + 1 < chips)
 
     def at_distance(distance, carry):
-        forward(distance, 0)
         early = (distance == 1) | jnp.logical_not(between)
         sides = [(where, there) for where, there, _, _ in sides_at(distance)]
         for where, there in sides:
@@ -260,14 +260,41 @@
             def _():
                 from_sibling(where)
 
-        for where, there in sides:
-            @pl.when(there)
-            def _():
-                finish(where, False)
+        (first, first_there), (second, second_there) = sides
+
+        @pl.when(first_there)
+        def _():
+            finish(first, False)
+
+        @pl.when(between)
+        def _():
+            forward(distance + 1, 0)
+
+        @pl.when(second_there)
+        def _():
+            finish(second, False)
+
+        @pl.when(jnp.logical_not(between))
+        def _():
+            forward(distance + 1, 0)
 
         return carry
 
+    forward(1, 0)
     lax.fori_loop(1, chips, at_distance, 0)
+
+    row16 = lax.broadcasted_iota(jnp.int32, (16, 128), 0)
+    lane16 = lax.broadcasted_iota(jnp.int32, (16, 128), 1)
+
+    def pick(row, lane):
+        return jnp.where((row16 == row) & (lane16 == lane), 1.0, 0.0).astype(jnp.bfloat16)
+
+    head = transposed_dot(pick(0, 0), image[:, 0:128].astype(jnp.bfloat16)) + transposed_dot(pick(1, 0), image[:, azimuths:azimuths + 128].astype(jnp.bfloat16))
+    column[0] = head[0:8]
+    send_column = push(
+        column.at[0], column.at[1], column_sem.at[0], column_sem.at[1], {"az": lax.rem(az + n_az - 1, n_az)}
+    )
+    send_column.start()
 
     def one_group(k, carry):
         cross_re, cross_im, power = carry
@@ -292,18 +319,10 @@
     zero = jnp.zeros((8, azimuths), jnp.float32)
     cross_re, cross_im, power = lax.fori_loop(0, cells // 16, one_group, (zero, zero, zero), unroll=2)
 
-    row16 = lax.broadcasted_iota(jnp.int32, (16, 128), 0)
-    lane16 = lax.broadcasted_iota(jnp.int32, (16, 128), 1)
-
-    def pick(row, lane):
-        return jnp.where((row16 == row) & (lane16 == lane), 1.0, 0.0).astype(jnp.bfloat16)
-
-    head = transposed_dot(pick(0, 0), out_re[:, 0:128]) + transposed_dot(pick(1, 0), out_im[:, 0:128])
-    column[0] = head[0:8]
-    send_column = push(
-        column.at[0], column.at[1], column_sem.at[0], column_sem.at[1], {"az": lax.rem(az + n_az - 1, n_az)}
-    )
-    send_column.start()
+    give_re = pltpu.make_async_copy(out_re, given_re, load_sem.at[0])
+    give_im = pltpu.make_async_copy(out_im, given_im, load_sem.at[1])
+    give_re.start()
+    give_im.start()
     tail_re = transposed_dot(pick(0, 127), out_re[:, azimuths - 128:])
     tail_im = transposed_dot(pick(0, 127), out_im[:, azimuths - 128:])
     send_column.wait_recv()
@@ -367,6 +386,8 @@
     turn_of[0] = jnp.cos(angle)
     turn_of[1] = jnp.sin(angle)
 
+    give_re.wait()
+    give_im.wait()
     send_column.wait_send()
     for turn in range(1, n_rng):
         send_sums(turn).wait_send()
@@ -404,13 +425,15 @@
 def turned(turn_of, in_re, in_im, out, mixed):
     lines, azimuths = in_re.shape
     tiles = azimuths // 128
+    pitch = 2 * tiles + 1
     for t in range(tiles):
         lanes = slice(t * 128, (t + 1) * 128)
         cosine, sine = turn_of[0, 0:1, lanes], turn_of[1, 0:1, lanes]
         re, im = in_re[:, lanes].astype(jnp.float32), in_im[:, lanes].astype(jnp.float32)
-        mixed[pl.ds(2 * t, lines, stride=2 * tiles), :] = re * cosine + im * sine
-        mixed[pl.ds(2 * t + 1, lines, stride=2 * tiles), :] = im * cosine - re * sine
-    out[...] = mixed[...].astype(jnp.bfloat16)
+        mixed[pl.ds(2 * t, lines, stride=pitch), :] = re * cosine + im * sine
+        mixed[pl.ds(2 * t + 1, lines, stride=pitch), :] = im * cosine - re * sine
+    for r in range(lines):
+        out[r * 2 * tiles:(r + 1) * 2 * tiles, :] = mixed[r * pitch:r * pitch + 2 * tiles, :].astype(jnp.bfloat16)
 
 
 def per_device(echoes, owner_map, band_start, interp, steer_phase):
@@ -431,8 +454,10 @@
         functools.partial(kernel, n_rng, n_az, pings, blocks),
         out_shape=(part, part, jax.ShapeDtypeStruct((2, 8, azimuths), jnp.float32)),
         in_specs=[smem, smem, anywhere, anywhere, anywhere],
-        out_specs=(vmem, vmem, vmem),
+        out_specs=(anywhere, anywhere, vmem),
         scratch_shapes=[
+            pltpu.VMEM((cells, azimuths), jnp.bfloat16),
+            pltpu.VMEM((cells, azimuths), jnp.bfloat16),
             pltpu.VMEM((n_az, rows, width + 2 * GUARD), jnp.bfloat16),
             pltpu.VMEM(interp.shape, jnp.bfloat16),
             pltpu.VMEM(steer_phase.shape, jnp.float32),
@@ -459,7 +484,7 @@
         out_shape=jax.ShapeDtypeStruct((cells * 2 * tiles, 128), jnp.bfloat16),
         in_specs=[pl.BlockSpec((2, 8, azimuths), lambda i: (0, 0, 0)), piece, piece],
         out_specs=pl.BlockSpec((lines * 2 * tiles, 128), lambda i: (i, 0)),
-        scratch_shapes=[pltpu.VMEM((lines * 2 * tiles, 128), jnp.float32)],
+        scratch_shapes=[pltpu.VMEM((lines * (2 * tiles + 1), 128), jnp.float32)],
     )(turn_of, re, im)
     mixed = mixed.reshape(cells, tiles, 2, 128)
     return jnp.transpose(mixed, (0, 2, 1, 3)).reshape(cells, 2, azimuths)

time: 69.9 us -> 63.5 us (0.908)
  Pallas kernels: 69.6 us -> 63.2 us
    pallas_call x1, Pallas kernels: 62.5 us -> 57.4 us  [per_device(): pl.pallas_call(functools.partial(kernel, n_rng, n_az, pings, blocks), out...]
    pallas_call x1, Pallas kernels: 7.11 us -> 5.84 us  [per_device(): pl.pallas_call(turned, grid=(cells // lines,), out_shape=jax.ShapeDtypeSt...]
where the time goes in v5:
time: 63.5 us; the launch traced here: 63.2 us
  Pallas kernels  63.2 us (100%)
    pallas_call x1, Pallas kernels, per_device(): pl.pallas_call(functools.partial(kernel, n_rng, n_az, pings, blocks), out...  57.4 us
    pallas_call x1, Pallas kernels, per_device(): pl.pallas_call(turned, grid=(cells // lines,), out_shape=jax.ShapeDtypeSt...  5.84 us

profile of v5, /device:TPU:0, one launch (start us, length us, event | category | flops | bytes accessed | tf_op | source)
XLA Modules:
  0.0 63.2 jit_solution(4735553171956320856)
XLA Ops:
  0.0 57.4 %shard_map.55 = (bf16[768,1024]{1,0:T(8,128)(2,1)}, bf16[768,1024]{1,0:T(8,128)(2,1)}, f32[2,8,1024]{2,1,0:T(8,128)}) custom-call(s32[8]{0:T(128)} %owner.1, s32[6,1,8]{2,1,0:T(1,128)} %start.1, bf16[128,1536]{1,0:T(8,128)(2,1)} %bitcast.8, bf16[8,768,256]{2,1,0:T(8,128)(2,1)} %bitcast.7, f32[8,64,1024]{2,1,0:T(8,128)} %phase.1), custom_call_target="tpu_custom_call" | custom-call | tf_op jit(solution)/shard_map/pallas_call | solution.py:453
  57.4 5.8 %shard_map.56 = bf16[12288,128]{1,0:T(8,128)(2,1)} custom-call(f32[2,8,1024]{2,1,0:T(8,128)} %get-tuple-element.8.turn_of, bf16[768,1024]{1,0:T(8,128)(2,1)} %get-tuple-element.9.in_re, bf16[768,1024]{1,0:T(8,128)(2,1)} %get-tuple-element.10.in_im), custom_call_target="tpu_custom_call" | custom-call | tf_op jit(solution)/shard_map/pallas_call | solution.py:481

commit v6 on v5

--- a/solution.py
+++ b/solution.py
@@ -13,21 +13,26 @@
 HALVES = 2
 
 
+SINE = (
+    1.0, -0.1666666716337204, 0.00833333283662796, -0.00019841254106722772, 2.7556704935705056e-06,
+    -2.50387266476082e-08, 1.5896819971494835e-10, -6.611164523814828e-13,
+)
+COSINE = (
+    1.0, -0.5, 0.0416666679084301, -0.00138888880610466, 2.4801563995424658e-05, -2.7556652071325516e-07,
+    2.0865218441912248e-09, -1.1353691424520473e-11, 4.131706099214788e-14,
+)
+
+
+def series(terms, u):
+    total = terms[-1] * u + terms[-2]
+    for term in terms[-3::-1]:
+        total = total * u + term
+    return total
+
+
 def sine_cosine(x):
-    turns = jnp.floor(x * 0.6366197723675814 + 0.5)
-    r = x - turns * 1.5703125
-    r = r - turns * 4.837512969970703e-4
-    r = r - turns * 7.549789948768648e-8
-    quadrant = turns.astype(jnp.int32)
-    r2 = r * r
-    s = r + r * r2 * (-1 / 6 + r2 * (1 / 120 + r2 * (-1 / 5040 + r2 * (1 / 362880))))
-    c = 1.0 + r2 * (-0.5 + r2 * (1 / 24 + r2 * (-1 / 720 + r2 * (1 / 40320))))
-    odd = (quadrant & 1) == 1
-    sine = jnp.where(odd, c, s)
-    cosine = jnp.where(odd, s, c)
-    sine = jnp.where((quadrant & 2) == 2, -sine, sine)
-    cosine = jnp.where(((quadrant + 1) & 2) == 2, -cosine, cosine)
-    return sine, cosine
+    square = x * x
+    return x * series(SINE, square), series(COSINE, square)
 
 
 def transposed_dot(a, b):
@@ -238,11 +243,12 @@
     prepare(chip)
     own_copy.wait()
     from_sibling(chip)
+    forward(1, 0)
     finish(chip, True)
     between = (chip > 0) & (chip + 1 < chips)
 
     def at_distance(distance, carry):
-        early = (distance == 1) | jnp.logical_not(between)
+        early = jnp.logical_not(between)
         sides = [(where, there) for where, there, _, _ in sides_at(distance)]
         for where, there in sides:
             @pl.when(there & early)
@@ -280,7 +286,6 @@
 
         return carry
 
-    forward(1, 0)
     lax.fori_loop(1, chips, at_distance, 0)
 
     row16 = lax.broadcasted_iota(jnp.int32, (16, 128), 0)

time: 63.5 us -> 63.1 us (level)
  no operation moved by 1% of the time
where the time goes in v6:
time: 63.1 us; the launch traced here: 62.9 us
  Pallas kernels  62.9 us (100%)
    pallas_call x1, Pallas kernels, per_device(): pl.pallas_call(functools.partial(kernel, n_rng, n_az, pings, blocks), out...  57 us
    pallas_call x1, Pallas kernels, per_device(): pl.pallas_call(turned, grid=(cells // lines,), out_shape=jax.ShapeDtypeSt...  5.84 us

profile of v6, /device:TPU:0, one launch (start us, length us, event | category | flops | bytes accessed | tf_op | source)
XLA Modules:
  0.0 62.9 jit_solution(11811409897853957789)
XLA Ops:
  0.0 57.0 %shard_map.55 = (bf16[768,1024]{1,0:T(8,128)(2,1)}, bf16[768,1024]{1,0:T(8,128)(2,1)}, f32[2,8,1024]{2,1,0:T(8,128)}) custom-call(s32[8]{0:T(128)} %owner.1, s32[6,1,8]{2,1,0:T(1,128)} %start.1, bf16[128,1536]{1,0:T(8,128)(2,1)} %bitcast.8, bf16[8,768,256]{2,1,0:T(8,128)(2,1)} %bitcast.7, f32[8,64,1024]{2,1,0:T(8,128)} %phase.1), custom_call_target="tpu_custom_call" | custom-call | tf_op jit(solution)/shard_map/pallas_call | solution.py:458
  57.0 5.8 %shard_map.56 = bf16[12288,128]{1,0:T(8,128)(2,1)} custom-call(f32[2,8,1024]{2,1,0:T(8,128)} %get-tuple-element.8.turn_of, bf16[768,1024]{1,0:T(8,128)(2,1)} %get-tuple-element.9.in_re, bf16[768,1024]{1,0:T(8,128)(2,1)} %get-tuple-element.10.in_im), custom_call_target="tpu_custom_call" | custom-call | tf_op jit(solution)/shard_map/pallas_call | solution.py:486

commit v7 on v6

--- a/solution.py
+++ b/solution.py
@@ -355,6 +355,34 @@
 
     for turn in range(1, n_rng):
         send_sums(turn).start()
+
+    def ended(slot, carry):
+        where = slot // 2
+        for part in range(HALVES):
+            @pl.when(slot % 2 == core)
+            def _():
+                along(inner(slot), slot, SIBLING, part).wait_send()
+
+                @pl.when((where <= chip) & (chip + 1 < chips))
+                def _():
+                    along(inner(slot), slot, RIGHT, part).wait_send()
+
+                @pl.when((where >= chip) & (chip > 0))
+                def _():
+                    along(inner(slot), slot, LEFT, part).wait_send()
+
+        @pl.when(rng + 1 < n_rng)
+        def _():
+            edge_low(inner(slot), slot).wait_send()
+
+        @pl.when(rng > 0)
+        def _():
+            edge_high(inner(slot), slot).wait_send()
+
+        return carry
+
+    lax.fori_loop(0, n_az, ended, 0)
+
     for turn in range(1, n_rng):
         take_sums(turn).wait_recv()
     total = sums[0]
@@ -382,14 +410,16 @@
 
     for turn in range(1, n_az):
         send_total(turn).start()
+    angle = running - slope
+    cosine, sine = jnp.cos(angle), jnp.sin(angle)
     for turn in range(1, n_az):
         take_total(turn).wait_recv()
     offset = jnp.zeros((8, 128), jnp.float32)
     for place in range(n_az):
         offset = offset + jnp.where(place < az, totals[place], 0.0)
-    angle = offset[:, 0:1] + running - slope
-    turn_of[0] = jnp.cos(angle)
-    turn_of[1] = jnp.sin(angle)
+    offset_cosine, offset_sine = jnp.cos(offset)[:, 0:1], jnp.sin(offset)[:, 0:1]
+    turn_of[0] = cosine * offset_cosine - sine * offset_sine
+    turn_of[1] = sine * offset_cosine + cosine * offset_sine
 
     give_re.wait()
     give_im.wait()
@@ -398,33 +428,6 @@
         send_sums(turn).wait_send()
     for turn in range(1, n_az):
         send_total(turn).wait_send()
-
-    def ended(slot, carry):
-        where = slot // 2
-        for part in range(HALVES):
-            @pl.when(slot % 2 == core)
-            def _():
-                along(inner(slot), slot, SIBLING, part).wait_send()
-
-                @pl.when((where <= chip) & (chip + 1 < chips))
-                def _():
-                    along(inner(slot), slot, RIGHT, part).wait_send()
-
-                @pl.when((where >= chip) & (chip > 0))
-                def _():
-                    along(inner(slot), slot, LEFT, part).wait_send()
-
-        @pl.when(rng + 1 < n_rng)
-        def _():
-            edge_low(inner(slot), slot).wait_send()
-
-        @pl.when(rng > 0)
-        def _():
-            edge_high(inner(slot), slot).wait_send()
-
-        return carry
-
-    lax.fori_loop(0, n_az, ended, 0)
 
 
 def turned(turn_of, in_re, in_im, out, mixed):

time: 63.1 us -> 62.9 us (level)
  no operation moved by 1% of the time
where the time goes in v7:
time: 62.9 us; the launch traced here: 62.6 us
  Pallas kernels  62.6 us (100%)
    pallas_call x1, Pallas kernels, per_device(): pl.pallas_call(functools.partial(kernel, n_rng, n_az, pings, blocks), out...  56.8 us
    pallas_call x1, Pallas kernels, per_device(): pl.pallas_call(turned, grid=(cells // lines,), out_shape=jax.ShapeDtypeSt...  5.84 us

profile of v7, /device:TPU:0, one launch (start us, length us, event | category | flops | bytes accessed | tf_op | source)
XLA Modules:
  0.0 62.6 jit_solution(5321117597195881110)
XLA Ops:
  0.0 56.8 %shard_map.55 = (bf16[768,1024]{1,0:T(8,128)(2,1)}, bf16[768,1024]{1,0:T(8,128)(2,1)}, f32[2,8,1024]{2,1,0:T(8,128)}) custom-call(s32[8]{0:T(128)} %owner.1, s32[6,1,8]{2,1,0:T(1,128)} %start.1, bf16[128,1536]{1,0:T(8,128)(2,1)} %bitcast.8, bf16[8,768,256]{2,1,0:T(8,128)(2,1)} %bitcast.7, f32[8,64,1024]{2,1,0:T(8,128)} %phase.1), custom_call_target="tpu_custom_call" | custom-call | tf_op jit(solution)/shard_map/pallas_call | solution.py:461
  56.8 5.8 %shard_map.56 = bf16[12288,128]{1,0:T(8,128)(2,1)} custom-call(f32[2,8,1024]{2,1,0:T(8,128)} %get-tuple-element.8.turn_of, bf16[768,1024]{1,0:T(8,128)(2,1)} %get-tuple-element.9.in_re, bf16[768,1024]{1,0:T(8,128)(2,1)} %get-tuple-element.10.in_im), custom_call_target="tpu_custom_call" | custom-call | tf_op jit(solution)/shard_map/pallas_call | solution.py:489
